TPU v7x, 256 devices: a whole 4x4x8 slice. The times are simulated.
256 devices in a mesh: row: 16 (over y, x_lo, core), col: 16 (over z, x_hi).
Axes of the slice: x: 4 (x_hi: 2, x_lo: 2; x = x_hi * 2 + x_lo), y: 4, z: 8, core: 2. Of those that a mesh axis runs over, the one named last changes fastest.
Arguments:
- node_feats: bfloat16 [524288, 128], P(('row', 'col')), may hold values from -6 to 6
- tile_vals: bfloat16 [16, 16, 256, 128, 128], P('row', 'col'), as said below
- tile_dest: int32 [16, 16, 256], P('row', 'col'), may hold values from 0 to 255, as said below
- tile_source: int32 [16, 16, 256], P('row', 'col'), may hold values from 0 to 255, as said below
- tile_count: int32 [16, 16], P('row', 'col'), may hold values from 32 to 256, as said below
- weight: bfloat16 [128, 256], replicated, may hold values from -0.5 to 0.5
- out_bias: float32 [256], replicated, may hold values from -3 to 3
Outputs:
- layer_out: bfloat16 [524288, 256], P(('row', 'col'))
Inputs may be any that keep to these rules, and one draw needn't show every extreme that they name: `tile_count`: busiest device holds exactly 256 live tiles in every draw; the loads follow a power law. `tile_dest`: 0 in slots at or past the device's count. The live tiles of one device touch at most 8 distinct destination blocks among the 16 blocks of each index of col, and some device touches exactly that many in every one of them. `tile_source`: 0 in slots at or past the device's count. `tile_vals`: Nonnegative; slots at or past the device's count hold stale values that are not part of A.
All inputs are finite; a program needn't handle non-finite values.
Results may differ from a plain program's by a relative error of at most 0.0047.
Values may be sent and summed in bfloat16 or wider, within the bound.
No kernel may reach another device: no remote copies, remote signals or barrier semaphores. Data moves between devices by JAX's collectives and lax.ppermute only.
A program may use at most 128 MiB of HBM per device.

v0:
```python
import functools

import jax
import jax.numpy as jnp
from jax import lax
from jax.experimental import pallas as pl
from jax.experimental.pallas import tpu as pltpu
from jax.sharding import PartitionSpec as P

TILE = 128
TPD = 16
SLOTS = 256
NY, NXLO, NCORE = 4, 2, 2
NZ, NXHI = 8, 2
ROWS = TPD * TILE
HALF_SLOTS = 8
OWN_BLOCKS = NZ * TPD
OTHER_BLOCKS = NZ * HALF_SLOTS
GROUP = 16
WIDTH = 512
CLASSES = 5
KINDS = 16
PACKED = ((0, 0), (1, 0), (3, 0), (0, 1), (2, 0), (3, 1), (1, 1), (2, 1))
EARLY = 4
LAST = 7
X_PARTS = ((4,), (3, 5), (2, 6), (1, 7), (0,))
THIRDS = (752, 880, 416)

VMEM = pltpu.VMEM
SMEM_SPEC = pl.BlockSpec(memory_space=pltpu.SMEM)
VMEM_SPEC = pl.BlockSpec(memory_space=pltpu.VMEM)
ANY_SPEC = pl.BlockSpec(memory_space=pl.ANY)


def row_perm(change):
    pairs = []
    for y in range(NY):
        for x in range(NXLO):
            for k in range(NCORE):
                ty, tx, tk = change(y, x, k)
                pairs.append(((y * NXLO + x) * NCORE + k, (ty % NY * NXLO + tx) * NCORE + tk))
    return pairs


FROM_UP = row_perm(lambda y, x, k: (y - 1, x, k))
FROM_DOWN = row_perm(lambda y, x, k: (y + 1, x, k))
FROM_SIDE = row_perm(lambda y, x, k: (y, 1 - x, k))
FROM_CORE = row_perm(lambda y, x, k: (y, x, 1 - k))
Z_PLUS = [(z * NXHI + x, (z + 1) % NZ * NXHI + x) for z in range(NZ) for x in range(NXHI)]
Z_MINUS = [(z * NXHI + x, (z - 1) % NZ * NXHI + x) for z in range(NZ) for x in range(NXHI)]
Z_CHAINS = (Z_PLUS, Z_MINUS)
X_FLIP = [(z * NXHI + x, z * NXHI + 1 - x) for z in range(NZ) for x in range(NXHI)]


def call(kernel, name, **kwargs):
    return pl.pallas_call(
        kernel,
        name=name,
        cost_estimate=pl.CostEstimate(flops=0, bytes_accessed=0, transcendentals=0),
        compiler_params=pltpu.CompilerParams(vmem_limit_bytes=16 << 20),
        **kwargs,
    )


def keep_scalars(array):
    return pltpu.with_memory_space_constraint(array, pltpu.SMEM)


def keep(array):
    return pltpu.with_memory_space_constraint(array, pltpu.VMEM)


def iota(shape, dim):
    return lax.broadcasted_iota(jnp.int32, shape, dim)


def to_column(row):
    n = row.shape[1]
    square = jnp.broadcast_to(row, (n, n))
    return jnp.sum(jnp.where(iota((n, n), 0) == iota((n, n), 1), square, 0.0), 1, keepdims=True)


def to_row(column):
    n = column.shape[0]
    square = jnp.broadcast_to(column, (n, n))
    return jnp.sum(jnp.where(iota((n, n), 0) == iota((n, n), 1), square, 0.0), 0, keepdims=True)


def split_dest(block, my_z):
    block = jnp.maximum(block, 0)
    away = ((block // (NXHI * TPD)) - my_z) & (NZ - 1)
    return away, (block // TPD) & (NXHI - 1), block & (TPD - 1)


def slots_of(key, chosen):
    hit = (iota((OWN_BLOCKS, SLOTS), 0) == key) & chosen
    touched = jnp.max(jnp.where(hit, 1.0, 0.0), axis=1, keepdims=True)
    a, b = iota((OWN_BLOCKS, OWN_BLOCKS), 0), iota((OWN_BLOCKS, OWN_BLOCKS), 1)
    before = (b < a) & (b // TPD == a // TPD)
    rank = jnp.sum(jnp.where(before, to_row(touched), 0.0), axis=1, keepdims=True)
    return hit, touched, rank


def lists_of(kind, value):
    kinds = iota((KINDS, SLOTS), 0)
    n = jnp.sum(jnp.where(kinds == kind, 1, 0).astype(jnp.float32), axis=1, keepdims=True)
    groups = jnp.floor((n + (GROUP - 1)) * (1.0 / GROUP))
    first = jnp.sum(jnp.where(kinds < kind, groups, 0.0), axis=0, keepdims=True) * GROUP
    kind_column = to_column(kind.astype(jnp.float32))
    earlier = iota((SLOTS, SLOTS), 0) < iota((SLOTS, SLOTS), 1)
    same = (kind_column == kind.astype(jnp.float32)) & earlier
    at = first + jnp.sum(jnp.where(same, 1.0, 0.0), axis=0, keepdims=True)
    at = to_column(jnp.where(kind < KINDS, at, -1.0))
    held = at == iota((SLOTS, WIDTH), 1).astype(jnp.float32)
    filled = jnp.sum(jnp.where(held, 1.0, 0.0), axis=0, keepdims=True)
    value = to_column(value.astype(jnp.float32))
    row = jnp.sum(jnp.where(held, value, 0.0), axis=0, keepdims=True).astype(jnp.int32)
    a, b = iota((KINDS, TILE), 0), iota((KINDS, TILE), 1)
    starts = jnp.sum(jnp.where(a < b, groups, 0.0), axis=0, keepdims=True)
    counts = jnp.sum(jnp.where(a == b, groups, 0.0), axis=0, keepdims=True)
    others = jnp.sum(jnp.where(iota((KINDS, 1), 0) < CLASSES, groups, 0.0)) * GROUP
    is_other = iota((1, WIDTH), 1).astype(jnp.float32) < others
    spare = jnp.where(is_other, OTHER_BLOCKS, OWN_BLOCKS) * 65536
    return jnp.where(filled > 0, row, spare), starts.astype(jnp.int32), counts.astype(jnp.int32)


def plan_kernel(where, dest, source, plan):
    my_y, my_x, my_k, my_z, my_xhi = (where[i] for i in range(5))
    block, from_block = dest[...], source[...]
    row = from_block // TPD
    rel = (((row // (NXLO * NCORE)) - my_y) & (NY - 1)) * NXLO
    rel = rel + (((row // NCORE) - my_x) & (NXLO - 1))
    sibling = (row - my_k) & (NCORE - 1)
    slot = jnp.zeros_like(rel)
    for i, (y, x) in enumerate(PACKED):
        slot = jnp.where(rel == y * NXLO + x, i, slot)
    is_far = slot == LAST
    feat = jnp.where(is_far, 0, slot) * TPD + (from_block & (TPD - 1))
    late = jnp.where(slot < EARLY, 0, 1)
    group = jnp.where(is_far, 3 + sibling, jnp.where(sibling == 1, 2, late))
    away, half, inner = split_dest(block, my_z)
    key = away * TPD + inner
    is_own = half == my_xhi
    live = block >= 0
    hit, _, rank = slots_of(key, live & (half != my_xhi))
    slot = jnp.sum(jnp.where(hit, rank, 0.0), axis=0, keepdims=True).astype(jnp.int32)
    to = jnp.where(is_own, key, away * HALF_SLOTS + slot)
    kind = jnp.where(live, jnp.where(is_own, CLASSES, 0) + group, KINDS)
    value = iota((1, SLOTS), 1) + feat * 256 + to * 65536
    row, starts, counts = lists_of(kind, value)
    plan[0:1, :] = row
    plan[1:2, 0:TILE] = starts
    plan[2:3, 0:TILE] = counts


def make_plan(where, dest, source):
    return call(
        plan_kernel,
        "plan",
        out_shape=jax.ShapeDtypeStruct((8, WIDTH), jnp.int32),
        in_specs=[SMEM_SPEC] + [VMEM_SPEC] * 2,
        out_specs=VMEM_SPEC,
    )(where, dest, source)


def map_kernel(where, partner_dest, slots, found, sem):
    my_z, my_xhi = where[3], where[4]
    block = partner_dest[...]
    away, half, inner = split_dest(block, my_z)
    _, touched, rank = slots_of(away * TPD + inner, (block >= 0) & (half == my_xhi))
    slot = to_row(jnp.where(touched > 0, rank, float(HALF_SLOTS)))
    found[...] = slot.astype(jnp.int32)
    copy = pltpu.make_async_copy(found, slots, sem)
    copy.start()
    copy.wait()


def make_map(where, partner_dest):
    return call(
        map_kernel,
        "partner_map",
        out_shape=pltpu.SMEM((1, OWN_BLOCKS), jnp.int32),
        in_specs=[SMEM_SPEC, VMEM_SPEC],
        out_specs=SMEM_SPEC,
        scratch_shapes=[VMEM((1, OWN_BLOCKS), jnp.int32), pltpu.SemaphoreType.DMA(())],
    )(where, partner_dest)


def add_products(plan, kind, tiles, feats, acc):
    def one_group(g, _):
        entries = [plan[0, g * GROUP + i] for i in range(GROUP)]
        products = [
            jnp.dot(
                tiles[e & 255],
                feats[pl.ds(pl.multiple_of(((e >> 8) & 255) * TILE, TILE), TILE), :],
                preferred_element_type=jnp.float32,
            )
            for e in entries
        ]
        for e, product in zip(entries, products):
            acc[e >> 16] += product
        return 0

    first = plan[1, kind]
    lax.fori_loop(first, first + plan[2, kind], one_group, 0)


def clear_blocks(acc, n):
    def clear(i, _):
        acc[i] = jnp.zeros(acc.shape[1:], acc.dtype)
        return 0

    lax.fori_loop(0, n, clear, 0, unroll=4)


def load_tiles_kernel(tiles_hbm, tiles, sem):
    copy = pltpu.make_async_copy(tiles_hbm, tiles, sem)
    copy.start()
    copy.wait()


def load_tiles(tile_set):
    return call(
        load_tiles_kernel,
        "load_tiles",
        out_shape=VMEM(tile_set.shape, tile_set.dtype),
        in_specs=[ANY_SPEC],
        out_specs=VMEM_SPEC,
        scratch_shapes=[pltpu.SemaphoreType.DMA(())],
    )(tile_set)


def pack_kernel(has_base, first, *refs):
    packed = refs[-1]
    for i, ref in enumerate(refs[has_base:-1]):
        packed[pl.ds(first + i * ROWS, ROWS), :] = ref[...]


def pack(base, first, arrays):
    has_base = base is not None
    return call(
        functools.partial(pack_kernel, has_base, first),
        "pack",
        out_shape=VMEM((LAST * ROWS, arrays[0].shape[1]), arrays[0].dtype),
        in_specs=[VMEM_SPEC] * (has_base + len(arrays)),
        out_specs=VMEM_SPEC,
        input_output_aliases={0: 0} if has_base else {},
    )(*([keep(base)] if has_base else []), *arrays)


def join_kernel(*refs):
    at = 0
    for ref in refs[:-1]:
        refs[-1][pl.ds(at, ref.shape[0]), :] = ref[...]
        at += ref.shape[0]


def join(arrays):
    return call(
        join_kernel,
        "join",
        out_shape=VMEM((ROWS, arrays[0].shape[1]), arrays[0].dtype),
        in_specs=[VMEM_SPEC] * len(arrays),
        out_specs=VMEM_SPEC,
    )(*arrays)


def first_kernel(plan, tiles, feats, _, other, own):
    clear_blocks(other, OTHER_BLOCKS)
    clear_blocks(own, OWN_BLOCKS)
    add_products(plan, 0, tiles, feats, other)
    add_products(plan, CLASSES, tiles, feats, own)


def first_products(plan, tiles, feats):
    block = (TILE, feats.shape[1])
    return call(
        first_kernel,
        "first_products",
        out_shape=[
            VMEM(feats.shape, feats.dtype),
            VMEM((OTHER_BLOCKS + 1, *block), jnp.float32),
            VMEM((OWN_BLOCKS + 1, *block), jnp.float32),
        ],
        in_specs=[SMEM_SPEC] + [VMEM_SPEC] * 2,
        out_specs=[VMEM_SPEC] * 3,
        input_output_aliases={2: 0},
    )(plan, keep(tiles), keep(feats))


def more_kernel(kinds, n_feats, plan, tiles, *refs):
    feats, accs = refs[:n_feats], refs[-len(kinds) :]
    for acc, of_acc in zip(accs, kinds):
        for kind, at in of_acc:
            add_products(plan, kind, tiles, feats[at], acc)


def more_products(name, kinds, plan, tiles, feats, accs):
    n = 2 + len(feats)
    return call(
        functools.partial(more_kernel, kinds, len(feats)),
        name,
        out_shape=[VMEM(acc.shape, acc.dtype) for acc in accs],
        in_specs=[SMEM_SPEC] + [VMEM_SPEC] * (n - 1 + len(accs)),
        out_specs=[VMEM_SPEC] * len(accs),
        input_output_aliases={n + i: i for i in range(len(accs))},
    )(plan, keep(tiles), *[keep(f) for f in feats], *[keep(acc) for acc in accs])


def convert_sends(acc, parts, sends):
    for aways, send in zip(parts, sends):
        for i, away in enumerate(aways):
            blocks = acc[pl.ds(away * HALF_SLOTS, HALF_SLOTS)]
            send[pl.ds(i * HALF_SLOTS, HALF_SLOTS)] = blocks.astype(send.dtype)


def first_send_kernel(plan, tiles, far_sibling, _, acc, send):
    add_products(plan, 4, tiles, far_sibling, acc)
    convert_sends(acc, X_PARTS[:1], [send])


def sends_kernel(acc, *sends):
    convert_sends(acc, X_PARTS[1:], sends)


def make_sends(plan, tiles, far_sibling, acc):
    part = lambda p: VMEM((HALF_SLOTS * len(p), *acc.shape[1:]), jnp.bfloat16)
    acc, first = call(
        first_send_kernel,
        "first_send",
        out_shape=[VMEM(acc.shape, acc.dtype), part(X_PARTS[0])],
        in_specs=[SMEM_SPEC] + [VMEM_SPEC] * 3,
        out_specs=[VMEM_SPEC] * 2,
        input_output_aliases={3: 0},
    )(plan, keep(tiles), keep(far_sibling), keep(acc))
    rest = call(
        sends_kernel,
        "other_sends",
        out_shape=[part(p) for p in X_PARTS[1:]],
        in_specs=[VMEM_SPEC],
        out_specs=[VMEM_SPEC] * (len(X_PARTS) - 1),
    )(keep(acc))
    return [first, *rest]


def merged(away, first, slots, own, arrived, passed, i):
    total = own[away * TPD + i]
    for ref, at in passed:
        if at <= i < at + ref.shape[0]:
            total += ref[i - at].astype(jnp.float32)
    slot = slots[0, away * TPD + i]
    seen = (slot < HALF_SLOTS).astype(jnp.float32)
    block = arrived[first + jnp.minimum(slot, HALF_SLOTS - 1)]
    return total + block.astype(jnp.float32) * seen


def hop_kernel(parts, slots, own, arrived, *refs):
    passed, outs = refs[: -len(parts)], refs[-len(parts) :]
    for out, (away, first, n, at, pass_at) in zip(outs, parts):
        refs = [(passed[i], block) for i, block in pass_at]
        for i in range(n):
            total = merged(away, first, slots, own, arrived, refs, at + i)
            out[i] = total.astype(out.dtype)


def hop(name, parts, slots, own, arrived, passed=()):
    return call(
        functools.partial(hop_kernel, parts),
        name,
        out_shape=[VMEM((p[2], *own.shape[1:]), jnp.bfloat16) for p in parts],
        in_specs=[SMEM_SPEC] + [VMEM_SPEC] * (2 + len(passed)),
        out_specs=[VMEM_SPEC] * len(parts),
    )(keep_scalars(slots), keep(own), arrived, *passed)


def last_kernel(first, slots, own, arrived, passed_a, passed_b, weight, bias, out):
    passed = [(passed_a, 0), (passed_b, 0)]
    for i in range(TPD):
        total = merged(0, first, slots, own, arrived, passed, i).astype(jnp.bfloat16)
        hidden = jnp.dot(total, weight[...], preferred_element_type=jnp.float32) + bias[...]
        out[pl.ds(i * TILE, TILE), :] = jnp.maximum(hidden, 0.0).astype(out.dtype)


def last(slots, own, arrived, passed, weight, bias):
    part, first = arrived
    return call(
        functools.partial(last_kernel, first),
        "last",
        out_shape=jax.ShapeDtypeStruct((ROWS, weight.shape[1]), jnp.bfloat16),
        in_specs=[SMEM_SPEC] + [VMEM_SPEC] * (4 + len(passed)),
        out_specs=VMEM_SPEC,
    )(keep_scalars(slots), keep(own), part, *passed, weight, bias)


def send(array, perm):
    return lax.ppermute(array, "row", perm)


def on_device(node_feats, tile_vals, tile_dest, tile_source, tile_count, weight, out_bias):
    row, col = lax.axis_index("row"), lax.axis_index("col")
    where = jnp.stack(
        [row // (NXLO * NCORE), row // NCORE % NXLO, row % NCORE, col // NXHI, col % NXHI]
    ).astype(jnp.int32)
    slot = jnp.arange(SLOTS, dtype=jnp.int32)[None, :]
    dest = jnp.where(slot < tile_count[0, 0], tile_dest[0], -1)
    up, down, side = (send(node_feats, p) for p in (FROM_UP, FROM_DOWN, FROM_SIDE))
    plan = make_plan(where, dest, tile_source[0])
    up, down, side, plan = lax.optimization_barrier((up, down, side, plan))
    far, down_side, up_side = send(up, FROM_UP), send(side, FROM_DOWN), send(up, FROM_SIDE)
    tiles = load_tiles(tile_vals[0, 0])
    feats = pack(None, 0, [node_feats, up, down, side])
    feats, other, own = first_products(plan, tiles, feats)
    far, down_side, up_side, feats, other, own = lax.optimization_barrier(
        (far, down_side, up_side, feats, other, own)
    )
    partner_dest = lax.ppermute(dest, "col", X_FLIP)
    thirds, at = [], 0
    for n, array, perm in zip(
        THIRDS, (up_side, down_side, far), (FROM_UP, FROM_DOWN, FROM_SIDE)
    ):
        thirds.append(send(array[at : at + n], perm))
        at += n
    feats = pack(feats, EARLY * ROWS, [far, down_side, up_side])
    sibling = send(feats, FROM_CORE)
    kinds = (((1, 0),), ((CLASSES + 1, 0),))
    other, own = more_products("late_products", kinds, plan, tiles, [feats], [other, own])
    thirds, other, own, partner_dest = lax.optimization_barrier((thirds, other, own, partner_dest))
    slots = make_map(where, partner_dest)
    last_feats = join(thirds)
    far_sibling = send(last_feats, FROM_CORE)
    kinds = (((2, 0), (3, 1)),)
    (other,) = more_products("other_half", kinds, plan, tiles, [sibling, last_feats], [other])
    sends = make_sends(plan, tiles, far_sibling, other)
    arrived = {}
    for aways, part in zip(X_PARTS, sends):
        part = lax.ppermute(part, "col", X_FLIP)
        for i, away in enumerate(aways):
            arrived[away] = (part, i * HALF_SLOTS)
    kinds = (tuple((CLASSES + 2 + i, i) for i in range(3)),)
    rest = [sibling, last_feats, far_sibling]
    (own,) = more_products("own_half", kinds, plan, tiles, rest, [own])
    cut = TPD // 2
    parts = ((4, 0, cut, 0, ()), (4, 0, cut, cut, ()))
    chains = hop("hop_4", parts, slots, own, arrived[4][0])
    for a, b in ((3, 5), (2, 6), (1, 7)):
        chains = [lax.ppermute(c, "col", p) for c, p in zip(chains, Z_CHAINS)]
        at = (0, cut if a == 3 else 0)
        chains = [
            hop(
                f"hop_{away}",
                ((away, arrived[away][1], TPD, 0, ((0, at[i]),)),),
                slots,
                own,
                arrived[away][0],
                (c,),
            )[0]
            for i, (away, c) in enumerate(zip((a, b), chains))
        ]
    chains = [lax.ppermute(c, "col", p) for c, p in zip(chains, Z_CHAINS)]
    return last(slots, own, arrived[0], chains, weight, out_bias.reshape(1, -1))


def solution(mesh):
    return jax.shard_map(
        on_device,
        mesh=mesh,
        in_specs=(
            P(("row", "col"), None),
            P("row", "col", None, None, None),
            P("row", "col", None),
            P("row", "col", None),
            P("row", "col"),
            P(),
            P(),
        ),
        out_specs=P(("row", "col"), None),
        check_vma=False,
    )
```

profile of v0, /device:TPU:26, one launch (start us, length us, event | category | flops | bytes accessed | tf_op | source)
XLA Modules:
  0.0 113.1 jit_solution(8277073087682700351)
XLA Ops:
  0.0 0.2 collective-permute-start.1
  0.2 1.8 %collective-permute-start = (bf16[2048,128]{1,0:T(8,128)(2,1)}, bf16[2048,128]{1,0:T(8,128)(2,1)S(1)}, u32[]{:S(2)}, u32[]{:S(2)}) collective-permute-start(bf16[2048,128]{1,0:T(8,128)(2,1)} %refs_0_.1), channel_id=1, source_target_pairs={{0,192},{16,208},{32,224},{48,240},{64,0},{80,16},{96,32},{112,48}... | collective-permute-start | bytes 1572872 | tf_op jit(solution)/shard_map/ppermute | solution.py:396
  2.0 0.5 collective-permute-start.2
  3.2 0.1 stack.23.where
  3.3 0.7 compare_select_fusion.dest
  4.0 0.7 copy-done.4
  4.7 1.0 plan.1
  5.7 8.2 %collective-permute-done.1.refs_2_ = bf16[2048,128]{1,0:T(8,128)(2,1)S(1)} collective-permute-done((bf16[2048,128]{1,0:T(8,128)(2,1)}, bf16[2048,128]{1,0:T(8,128)(2,1)S(1)}, u32[]{:S(2)}, u32[]{:S(2)}) %collective-permute-start.1) | collective-permute-done | bytes 524320 | tf_op jit(solution)/shard_map/ppermute | solution.py:396
  13.9 1.2 %collective-permute-done.refs_1_ = bf16[2048,128]{1,0:T(8,128)(2,1)S(1)} collective-permute-done((bf16[2048,128]{1,0:T(8,128)(2,1)}, bf16[2048,128]{1,0:T(8,128)(2,1)S(1)}, u32[]{:S(2)}, u32[]{:S(2)}) %collective-permute-start) | collective-permute-done | bytes 524320 | tf_op jit(solution)/shard_map/ppermute | solution.py:396
  15.1 0.3 collective-permute-done.2.refs_3_
  15.3 1.5 %collective-permute-start.4 = (bf16[2048,128]{1,0:T(8,128)(2,1)S(1)}, bf16[2048,128]{1,0:T(8,128)(2,1)S(1)}, u32[]{:S(2)}, u32[]{:S(2)}) collective-permute-start(bf16[2048,128]{1,0:T(8,128)(2,1)S(1)} %collective-permute-done.2.refs_3_), channel_id=1, source_target_pairs={{0,64},{16,80},{32,96},{48,112},{64,128},{80,144},{96,160},{112,17... | collective-permute-start | bytes 1572872 | tf_op jit(solution)/shard_map/ppermute | solution.py:396
  16.8 0.5 collective-permute-start.5
  17.4 0.5 collective-permute-start.3
  17.9 3.4 %copy-done = bf16[1,1,256,128,128]{4,3,2,1,0:T(8,128)(2,1)S(1)} copy-done((bf16[1,1,256,128,128]{4,3,2,1,0:T(8,128)(2,1)S(1)}, bf16[1,1,256,128,128]{4,3,2,1,0:T(8,128)(2,1)}, u32[]{:S(2)}) %copy-start) | copy-done | bytes 8388632
  21.3 0.6 load_tiles.1.tiles
  21.9 0.5 copy-done.1
  22.3 0.1 pack.2.feats
  22.5 2.3 %first_products.1 = (bf16[14336,128]{1,0:T(8,128)(2,1)S(1)}, f32[65,128,128]{2,1,0:T(8,128)S(1)}, f32[129,128,128]{2,1,0:T(8,128)S(1)}) custom-call(s32[8,512]{1,0:T(8,128)S(1)} %plan.1, bf16[256,128,128]{2,1,0:T(8,128)(2,1)S(1)} %load_tiles.1.tiles, bf16[14336,128]{1,0:T(8,128)(2,1)S(1)} %pack.2.feats), custom_call_target="tpu_custom_call", output_to_operand_aliasing={{0}: (2, {})} | custom-call | tf_op jit(solution)/shard_map/first_products/pallas_call | solution.py:277
  24.8 2.8 %collective-permute-done.4.refs_2_ = bf16[2048,128]{1,0:T(8,128)(2,1)S(1)} collective-permute-done((bf16[2048,128]{1,0:T(8,128)(2,1)S(1)}, bf16[2048,128]{1,0:T(8,128)(2,1)S(1)}, u32[]{:S(2)}, u32[]{:S(2)}) %collective-permute-start.4) | collective-permute-done | bytes 524320 | tf_op jit(solution)/shard_map/ppermute | solution.py:396
  27.6 0.9 collective-permute-done.5.refs_3_
  28.5 1.2 %collective-permute-done.3.refs_1_ = bf16[2048,128]{1,0:T(8,128)(2,1)S(1)} collective-permute-done((bf16[2048,128]{1,0:T(8,128)(2,1)S(1)}, bf16[2048,128]{1,0:T(8,128)(2,1)S(1)}, u32[]{:S(2)}, u32[]{:S(2)}) %collective-permute-start.3) | collective-permute-done | bytes 524320 | tf_op jit(solution)/shard_map/ppermute | solution.py:396
  29.7 0.1 pack.3.refs_0_
  29.8 0.1 collective-permute-start.10
  30.0 0.4 collective-permute-start.7
  30.3 1.8 %collective-permute-start.6 = (bf16[752,128]{1,0:T(8,128)(2,1)S(1)}, bf16[752,128]{1,0:T(8,128)(2,1)S(1)}, u32[]{:S(2)}, u32[]{:S(2)}) collective-permute-start(bf16[752,128]{1,0:T(8,128)(2,1)S(1)} %slice.9), channel_id=1, source_target_pairs={{0,192},{16,208},{32,224},{48,240},{64,0},{80,16},{96,32},{112,48}... | collective-permute-start | bytes 577544 | tf_op jit(solution)/shard_map/ppermute | solution.py:396
  32.2 1.8 %collective-permute-start.8 = (bf16[416,128]{1,0:T(8,128)(2,1)S(1)}, bf16[416,128]{1,0:T(8,128)(2,1)S(1)}, u32[]{:S(2)}, u32[]{:S(2)}) collective-permute-start(bf16[416,128]{1,0:T(8,128)(2,1)S(1)} %slice.11), channel_id=1, source_target_pairs={{0,32},{16,48},{32,0},{48,16},{64,96},{80,112},{96,64},{112,80},{1... | collective-permute-start | bytes 319496 | tf_op jit(solution)/shard_map/ppermute | solution.py:396
  34.0 2.4 %collective-permute-start.9 = (s32[1,256]{1,0:T(1,128)S(1)}, s32[1,256]{1,0:T(1,128)S(1)}, u32[]{:S(2)}, u32[]{:S(2)}) collective-permute-start(s32[1,256]{1,0:T(1,128)S(1)} %compare_select_fusion.dest), channel_id=1, source_target_pairs={{0,1},{1,0},{2,3},{3,2},{4,5},{5,4},{6,7},{7,6},{8,9},{9,8},{10,11... | collective-permute-start | bytes 3080 | tf_op jit(solution)/shard_map/ppermute | solution.py:416
  36.4 1.4 %late_products.1 = (f32[65,128,128]{2,1,0:T(8,128)S(1)}, f32[129,128,128]{2,1,0:T(8,128)S(1)}) custom-call(s32[8,512]{1,0:T(8,128)S(1)} %plan.1, bf16[256,128,128]{2,1,0:T(8,128)(2,1)S(1)} %load_tiles.1.tiles, bf16[14336,128]{1,0:T(8,128)(2,1)S(1)} %pack.3.refs_0_, ...), custom_call_target="tpu_custom_call", output_to_operand_aliasing={{0}: (3, {}), {1}: (4, {})} | custom-call | tf_op jit(solution)/shard_map/late_products/pallas_call | solution.py:300
  37.8 1.4 %collective-permute-done.9.partner_dest = s32[1,256]{1,0:T(1,128)S(1)} collective-permute-done((s32[1,256]{1,0:T(1,128)S(1)}, s32[1,256]{1,0:T(1,128)S(1)}, u32[]{:S(2)}, u32[]{:S(2)}) %collective-permute-start.9) | collective-permute-done | bytes 1056 | tf_op jit(solution)/shard_map/ppermute | solution.py:416
  39.3 0.1 collective-permute-start.11
  39.4 1.4 %other_half.1._ = f32[65,128,128]{2,1,0:T(8,128)S(1)} custom-call(s32[8,512]{1,0:T(8,128)S(1)} %plan.1, bf16[256,128,128]{2,1,0:T(8,128)(2,1)S(1)} %load_tiles.1.tiles, bf16[14336,128]{1,0:T(8,128)(2,1)S(1)} %collective-permute-done.10.refs_0_, bf16[2048,128]{1,0:T(8,128)(2,1)S(1)} %join.1.refs_1_, ...), custom_call_target="tpu_custom_call", output_to_operand_aliasing={{}: (4, {})} | custom-call | tf_op jit(solution)/shard_map/other_half/pallas_call | solution.py:300
  40.8 0.5 collective-permute-done.11.refs_2_.far_sibling
  41.3 1.1 %first_send.1 = (f32[65,128,128]{2,1,0:T(8,128)S(1)}, bf16[8,128,128]{2,1,0:T(8,128)(2,1)S(1)}) custom-call(s32[8,512]{1,0:T(8,128)S(1)} %plan.1, bf16[256,128,128]{2,1,0:T(8,128)(2,1)S(1)} %load_tiles.1.tiles, bf16[2048,128]{1,0:T(8,128)(2,1)S(1)} %collective-permute-done.11.refs_2_.far_sibling, ...), custom_call_target="tpu_custom_call", output_to_operand_aliasing={{0}: (3, {})} | custom-call | tf_op jit(solution)/shard_map/first_send/pallas_call | solution.py:328
  42.4 0.2 other_sends.1
  42.6 2.4 %collective-permute-start.16 = (bf16[8,128,128]{2,1,0:T(8,128)(2,1)S(1)}, bf16[8,128,128]{2,1,0:T(8,128)(2,1)S(1)}, u32[]{:S(2)}, u32[]{:S(2)}) collective-permute-start(bf16[8,128,128]{2,1,0:T(8,128)(2,1)S(1)} %get-tuple-element.60), channel_id=1, source_target_pairs={{0,1},{1,0},{2,3},{3,2},{4,5},{5,4},{6,7},{7,6},{8,9},{9,8},{10,11... | collective-permute-start | bytes 786440 | tf_op jit(solution)/shard_map/ppermute | solution.py:436
  45.0 1.2 %collective-permute-start.15 = (bf16[16,128,128]{2,1,0:T(8,128)(2,1)S(1)}, bf16[16,128,128]{2,1,0:T(8,128)(2,1)S(1)}, u32[]{:S(2)}, u32[]{:S(2)}) collective-permute-start(bf16[16,128,128]{2,1,0:T(8,128)(2,1)S(1)} %get-tuple-element.59), channel_id=1, source_target_pairs={{0,1},{1,0},{2,3},{3,2},{4,5},{5,4},{6,7},{7,6},{8,9},{9,8},{10,11... | collective-permute-start | bytes 1572872 | tf_op jit(solution)/shard_map/ppermute | solution.py:436
  46.2 1.3 %partner_map.1.slots = s32[1,128]{1,0:T(1,128)S(4)} custom-call(s32[5]{0:T(128)S(1)} %stack.23.where, s32[1,256]{1,0:T(1,128)S(1)} %collective-permute-done.9.partner_dest), custom_call_target="tpu_custom_call" | custom-call | tf_op jit(solution)/shard_map/partner_map/pallas_call | solution.py:179
  47.5 1.7 %own_half.1.own = f32[129,128,128]{2,1,0:T(8,128)S(1)} custom-call(s32[8,512]{1,0:T(8,128)S(1)} %plan.1, bf16[256,128,128]{2,1,0:T(8,128)(2,1)S(1)} %load_tiles.1.tiles, bf16[14336,128]{1,0:T(8,128)(2,1)S(1)} %collective-permute-done.10.refs_0_, bf16[2048,128]{1,0:T(8,128)(2,1)S(1)} %join.1.refs_1_, ...), custom_call_target="tpu_custom_call", output_to_operand_aliasing={{}: (5, {})} | custom-call | tf_op jit(solution)/shard_map/own_half/pallas_call | solution.py:300
  49.3 4.1 %collective-permute-done.16.arrived = bf16[8,128,128]{2,1,0:T(8,128)(2,1)S(1)} collective-permute-done((bf16[8,128,128]{2,1,0:T(8,128)(2,1)S(1)}, bf16[8,128,128]{2,1,0:T(8,128)(2,1)S(1)}, u32[]{:S(2)}, u32[]{:S(2)}) %collective-permute-start.16) | collective-permute-done | bytes 262176 | tf_op jit(solution)/shard_map/ppermute | solution.py:436
  53.3 0.1 hop_4.1
  53.5 2.7 %collective-permute-start.17 = (bf16[8,128,128]{2,1,0:T(8,128)(2,1)S(1)}, bf16[8,128,128]{2,1,0:T(8,128)(2,1)S(1)}, u32[]{:S(2)}, u32[]{:S(2)}) collective-permute-start(bf16[8,128,128]{2,1,0:T(8,128)(2,1)S(1)} %get-tuple-element.61), channel_id=1, source_target_pairs={{0,2},{1,3},{2,4},{3,5},{4,6},{5,7},{6,8},{7,9},{8,10},{9,11},{10,... | collective-permute-start | bytes 786440 | tf_op jit(solution)/shard_map/ppermute | solution.py:446
  56.2 3.2 %collective-permute-start.21 = (bf16[8,128,128]{2,1,0:T(8,128)(2,1)S(1)}, bf16[8,128,128]{2,1,0:T(8,128)(2,1)S(1)}, u32[]{:S(2)}, u32[]{:S(2)}) collective-permute-start(bf16[8,128,128]{2,1,0:T(8,128)(2,1)S(1)} %get-tuple-element.62), channel_id=1, source_target_pairs={{0,14},{1,15},{2,0},{3,1},{4,2},{5,3},{6,4},{7,5},{8,6},{9,7},{10,... | collective-permute-start | bytes 786440 | tf_op jit(solution)/shard_map/ppermute | solution.py:446
  59.4 2.4 %collective-permute-start.14 = (bf16[16,128,128]{2,1,0:T(8,128)(2,1)S(1)}, bf16[16,128,128]{2,1,0:T(8,128)(2,1)S(1)}, u32[]{:S(2)}, u32[]{:S(2)}) collective-permute-start(bf16[16,128,128]{2,1,0:T(8,128)(2,1)S(1)} %get-tuple-element.58), channel_id=1, source_target_pairs={{0,1},{1,0},{2,3},{3,2},{4,5},{5,4},{6,7},{7,6},{8,9},{9,8},{10,11... | collective-permute-start | bytes 1572872 | tf_op jit(solution)/shard_map/ppermute | solution.py:436
  61.8 2.4 %collective-permute-done.15.arrived = bf16[16,128,128]{2,1,0:T(8,128)(2,1)S(1)} collective-permute-done((bf16[16,128,128]{2,1,0:T(8,128)(2,1)S(1)}, bf16[16,128,128]{2,1,0:T(8,128)(2,1)S(1)}, u32[]{:S(2)}, u32[]{:S(2)}) %collective-permute-start.15) | collective-permute-done | bytes 524320 | tf_op jit(solution)/shard_map/ppermute | solution.py:436
  64.2 1.6 %collective-permute-done.17.refs_0_ = bf16[8,128,128]{2,1,0:T(8,128)(2,1)S(1)} collective-permute-done((bf16[8,128,128]{2,1,0:T(8,128)(2,1)S(1)}, bf16[8,128,128]{2,1,0:T(8,128)(2,1)S(1)}, u32[]{:S(2)}, u32[]{:S(2)}) %collective-permute-start.17) | collective-permute-done | bytes 262176 | tf_op jit(solution)/shard_map/ppermute | solution.py:446
  65.8 0.2 hop_3.1
  66.0 1.5 %collective-permute-start.18 = (bf16[16,128,128]{2,1,0:T(8,128)(2,1)S(1)}, bf16[16,128,128]{2,1,0:T(8,128)(2,1)S(1)}, u32[]{:S(2)}, u32[]{:S(2)}) collective-permute-start(bf16[16,128,128]{2,1,0:T(8,128)(2,1)S(1)} %hop_3.1), channel_id=1, source_target_pairs={{0,2},{1,3},{2,4},{3,5},{4,6},{5,7},{6,8},{7,9},{8,10},{9,11},{10,... | collective-permute-start | bytes 1572872 | tf_op jit(solution)/shard_map/ppermute | solution.py:446
  67.5 0.2 hop_5.1
  67.6 3.2 %collective-permute-start.22 = (bf16[16,128,128]{2,1,0:T(8,128)(2,1)S(1)}, bf16[16,128,128]{2,1,0:T(8,128)(2,1)S(1)}, u32[]{:S(2)}, u32[]{:S(2)}) collective-permute-start(bf16[16,128,128]{2,1,0:T(8,128)(2,1)S(1)} %hop_5.1), channel_id=1, source_target_pairs={{0,14},{1,15},{2,0},{3,1},{4,2},{5,3},{6,4},{7,5},{8,6},{9,7},{10,... | collective-permute-start | bytes 1572872 | tf_op jit(solution)/shard_map/ppermute | solution.py:446
  70.8 2.4 %collective-permute-start.13 = (bf16[16,128,128]{2,1,0:T(8,128)(2,1)S(1)}, bf16[16,128,128]{2,1,0:T(8,128)(2,1)S(1)}, u32[]{:S(2)}, u32[]{:S(2)}) collective-permute-start(bf16[16,128,128]{2,1,0:T(8,128)(2,1)S(1)} %get-tuple-element.57), channel_id=1, source_target_pairs={{0,1},{1,0},{2,3},{3,2},{4,5},{5,4},{6,7},{7,6},{8,9},{9,8},{10,11... | collective-permute-start | bytes 1572872 | tf_op jit(solution)/shard_map/ppermute | solution.py:436
  73.2 2.0 %collective-permute-done.14.arrived = bf16[16,128,128]{2,1,0:T(8,128)(2,1)S(1)} collective-permute-done((bf16[16,128,128]{2,1,0:T(8,128)(2,1)S(1)}, bf16[16,128,128]{2,1,0:T(8,128)(2,1)S(1)}, u32[]{:S(2)}, u32[]{:S(2)}) %collective-permute-start.14) | collective-permute-done | bytes 524320 | tf_op jit(solution)/shard_map/ppermute | solution.py:436
  75.2 7.5 %collective-permute-done.18.refs_0_ = bf16[16,128,128]{2,1,0:T(8,128)(2,1)S(1)} collective-permute-done((bf16[16,128,128]{2,1,0:T(8,128)(2,1)S(1)}, bf16[16,128,128]{2,1,0:T(8,128)(2,1)S(1)}, u32[]{:S(2)}, u32[]{:S(2)}) %collective-permute-start.18) | collective-permute-done | bytes 524320 | tf_op jit(solution)/shard_map/ppermute | solution.py:446
  82.7 0.2 hop_2.1
  82.9 0.1 collective-permute-start.19
  83.0 0.2 hop_6.1
  83.2 3.3 %collective-permute-start.23 = (bf16[16,128,128]{2,1,0:T(8,128)(2,1)S(1)}, bf16[16,128,128]{2,1,0:T(8,128)(2,1)S(1)}, u32[]{:S(2)}, u32[]{:S(2)}) collective-permute-start(bf16[16,128,128]{2,1,0:T(8,128)(2,1)S(1)} %hop_6.1), channel_id=1, source_target_pairs={{0,14},{1,15},{2,0},{3,1},{4,2},{5,3},{6,4},{7,5},{8,6},{9,7},{10,... | collective-permute-start | bytes 1572872 | tf_op jit(solution)/shard_map/ppermute | solution.py:446
  86.5 11.1 %collective-permute-done.19.refs_0_ = bf16[16,128,128]{2,1,0:T(8,128)(2,1)S(1)} collective-permute-done((bf16[16,128,128]{2,1,0:T(8,128)(2,1)S(1)}, bf16[16,128,128]{2,1,0:T(8,128)(2,1)S(1)}, u32[]{:S(2)}, u32[]{:S(2)}) %collective-permute-start.19) | collective-permute-done | bytes 524320 | tf_op jit(solution)/shard_map/ppermute | solution.py:446
  97.6 0.2 hop_1.1
  97.8 0.1 collective-permute-start.20
  97.9 0.2 hop_7.1
  98.1 3.3 %collective-permute-start.24 = (bf16[16,128,128]{2,1,0:T(8,128)(2,1)S(1)}, bf16[16,128,128]{2,1,0:T(8,128)(2,1)S(1)}, u32[]{:S(2)}, u32[]{:S(2)}) collective-permute-start(bf16[16,128,128]{2,1,0:T(8,128)(2,1)S(1)} %hop_7.1), channel_id=1, source_target_pairs={{0,14},{1,15},{2,0},{3,1},{4,2},{5,3},{6,4},{7,5},{8,6},{9,7},{10,... | collective-permute-start | bytes 1572872 | tf_op jit(solution)/shard_map/ppermute | solution.py:459
  101.5 7.8 %collective-permute-done.12.arrived = bf16[8,128,128]{2,1,0:T(8,128)(2,1)S(1)} collective-permute-done((bf16[8,128,128]{2,1,0:T(8,128)(2,1)S(1)}, bf16[8,128,128]{2,1,0:T(8,128)(2,1)S(1)}, u32[]{:S(2)}, u32[]{:S(2)}) %collective-permute-start.12) | collective-permute-done | bytes 262176 | tf_op jit(solution)/shard_map/ppermute | solution.py:436
  109.3 2.3 %collective-permute-done.20.passed_a = bf16[16,128,128]{2,1,0:T(8,128)(2,1)S(1)} collective-permute-done((bf16[16,128,128]{2,1,0:T(8,128)(2,1)S(1)}, bf16[16,128,128]{2,1,0:T(8,128)(2,1)S(1)}, u32[]{:S(2)}, u32[]{:S(2)}) %collective-permute-start.20) | collective-permute-done | bytes 524320 | tf_op jit(solution)/shard_map/ppermute | solution.py:459
  111.6 1.5 %last.1 = bf16[2048,256]{1,0:T(8,128)(2,1)} custom-call(s32[1,128]{1,0:T(1,128)S(4)} %partner_map.1.slots, f32[129,128,128]{2,1,0:T(8,128)S(1)} %own_half.1.own, bf16[8,128,128]{2,1,0:T(8,128)(2,1)S(1)} %collective-permute-done.12.arrived, bf16[16,128,128]{2,1,0:T(8,128)(2,1)S(1)} %collective-permute-done.20.passed_a, ...), custom_call_target="tpu_custom_call" | custom-call | tf_op jit(solution)/shard_map/last/pallas_call | solution.py:386
  (21 shorter events, 0.2 us)
Async XLA Ops:
  0.0 13.9 %collective-permute-start.1 = (bf16[2048,128]{1,0:T(8,128)(2,1)}, bf16[2048,128]{1,0:T(8,128)(2,1)S(1)}, u32[]{:S(2)}, u32[]{:S(2)}) collective-permute-start(bf16[2048,128]{1,0:T(8,128)(2,1)} %refs_0_.1), channel_id=1, source_target_pairs={{0,64},{16,80},{32,96},{48,112},{64,128},{80,144},{96,160},{112,17... | collective-permute-start | bytes 1572872 | tf_op jit(solution)/shard_map/ppermute | solution.py:396
  0.2 14.9 %collective-permute-start = (bf16[2048,128]{1,0:T(8,128)(2,1)}, bf16[2048,128]{1,0:T(8,128)(2,1)S(1)}, u32[]{:S(2)}, u32[]{:S(2)}) collective-permute-start(bf16[2048,128]{1,0:T(8,128)(2,1)} %refs_0_.1), channel_id=1, source_target_pairs={{0,192},{16,208},{32,224},{48,240},{64,0},{80,16},{96,32},{112,48}... | collective-permute-start | bytes 1572872 | tf_op jit(solution)/shard_map/ppermute | solution.py:396
  2.0 13.3 %collective-permute-start.2 = (bf16[2048,128]{1,0:T(8,128)(2,1)}, bf16[2048,128]{1,0:T(8,128)(2,1)S(1)}, u32[]{:S(2)}, u32[]{:S(2)}) collective-permute-start(bf16[2048,128]{1,0:T(8,128)(2,1)} %refs_0_.1), channel_id=1, source_target_pairs={{0,32},{16,48},{32,0},{48,16},{64,96},{80,112},{96,64},{112,80},{1... | collective-permute-start | bytes 1572872 | tf_op jit(solution)/shard_map/ppermute | solution.py:396
  4.0 0.7 copy-start.4
  15.3 12.3 %collective-permute-start.4 = (bf16[2048,128]{1,0:T(8,128)(2,1)S(1)}, bf16[2048,128]{1,0:T(8,128)(2,1)S(1)}, u32[]{:S(2)}, u32[]{:S(2)}) collective-permute-start(bf16[2048,128]{1,0:T(8,128)(2,1)S(1)} %collective-permute-done.2.refs_3_), channel_id=1, source_target_pairs={{0,64},{16,80},{32,96},{48,112},{64,128},{80,144},{96,160},{112,17... | collective-permute-start | bytes 1572872 | tf_op jit(solution)/shard_map/ppermute | solution.py:396
  16.8 11.7 %collective-permute-start.5 = (bf16[2048,128]{1,0:T(8,128)(2,1)S(1)}, bf16[2048,128]{1,0:T(8,128)(2,1)S(1)}, u32[]{:S(2)}, u32[]{:S(2)}) collective-permute-start(bf16[2048,128]{1,0:T(8,128)(2,1)S(1)} %collective-permute-done.refs_1_), channel_id=1, source_target_pairs={{0,32},{16,48},{32,0},{48,16},{64,96},{80,112},{96,64},{112,80},{1... | collective-permute-start | bytes 1572872 | tf_op jit(solution)/shard_map/ppermute | solution.py:396
  17.4 12.4 %collective-permute-start.3 = (bf16[2048,128]{1,0:T(8,128)(2,1)S(1)}, bf16[2048,128]{1,0:T(8,128)(2,1)S(1)}, u32[]{:S(2)}, u32[]{:S(2)}) collective-permute-start(bf16[2048,128]{1,0:T(8,128)(2,1)S(1)} %collective-permute-done.refs_1_), channel_id=1, source_target_pairs={{0,192},{16,208},{32,224},{48,240},{64,0},{80,16},{96,32},{112,48}... | collective-permute-start | bytes 1572872 | tf_op jit(solution)/shard_map/ppermute | solution.py:396
  17.9 3.4 %copy-start = (bf16[1,1,256,128,128]{4,3,2,1,0:T(8,128)(2,1)S(1)}, bf16[1,1,256,128,128]{4,3,2,1,0:T(8,128)(2,1)}, u32[]{:S(2)}) copy-start(bf16[1,1,256,128,128]{4,3,2,1,0:T(8,128)(2,1)} %param.8) | copy-start | bytes 25165828
  21.3 1.0 copy-start.1
  29.8 9.5 %collective-permute-start.10 = (bf16[14336,128]{1,0:T(8,128)(2,1)S(1)}, bf16[14336,128]{1,0:T(8,128)(2,1)S(1)}, u32[]{:S(2)}, u32[]{:S(2)}) collective-permute-start(bf16[14336,128]{1,0:T(8,128)(2,1)S(1)} %pack.3.refs_0_), channel_id=1, source_target_pairs={{0,16},{16,0},{32,48},{48,32},{64,80},{80,64},{96,112},{112,96},{1... | collective-permute-start | bytes 11010056 | tf_op jit(solution)/shard_map/ppermute | solution.py:396
  30.0 9.3 %collective-permute-start.7 = (bf16[880,128]{1,0:T(8,128)(2,1)S(1)}, bf16[880,128]{1,0:T(8,128)(2,1)S(1)}, u32[]{:S(2)}, u32[]{:S(2)}) collective-permute-start(bf16[880,128]{1,0:T(8,128)(2,1)S(1)} %slice.10), channel_id=1, source_target_pairs={{0,64},{16,80},{32,96},{48,112},{64,128},{80,144},{96,160},{112,17... | collective-permute-start | bytes 675848 | tf_op jit(solution)/shard_map/ppermute | solution.py:396
  30.3 8.9 %collective-permute-start.6 = (bf16[752,128]{1,0:T(8,128)(2,1)S(1)}, bf16[752,128]{1,0:T(8,128)(2,1)S(1)}, u32[]{:S(2)}, u32[]{:S(2)}) collective-permute-start(bf16[752,128]{1,0:T(8,128)(2,1)S(1)} %slice.9), channel_id=1, source_target_pairs={{0,192},{16,208},{32,224},{48,240},{64,0},{80,16},{96,32},{112,48}... | collective-permute-start | bytes 577544 | tf_op jit(solution)/shard_map/ppermute | solution.py:396
  32.2 7.0 %collective-permute-start.8 = (bf16[416,128]{1,0:T(8,128)(2,1)S(1)}, bf16[416,128]{1,0:T(8,128)(2,1)S(1)}, u32[]{:S(2)}, u32[]{:S(2)}) collective-permute-start(bf16[416,128]{1,0:T(8,128)(2,1)S(1)} %slice.11), channel_id=1, source_target_pairs={{0,32},{16,48},{32,0},{48,16},{64,96},{80,112},{96,64},{112,80},{1... | collective-permute-start | bytes 319496 | tf_op jit(solution)/shard_map/ppermute | solution.py:396
  34.0 5.2 %collective-permute-start.9 = (s32[1,256]{1,0:T(1,128)S(1)}, s32[1,256]{1,0:T(1,128)S(1)}, u32[]{:S(2)}, u32[]{:S(2)}) collective-permute-start(s32[1,256]{1,0:T(1,128)S(1)} %compare_select_fusion.dest), channel_id=1, source_target_pairs={{0,1},{1,0},{2,3},{3,2},{4,5},{5,4},{6,7},{7,6},{8,9},{9,8},{10,11... | collective-permute-start | bytes 3080 | tf_op jit(solution)/shard_map/ppermute | solution.py:416
  39.3 2.0 %collective-permute-start.11 = (bf16[2048,128]{1,0:T(8,128)(2,1)S(1)}, bf16[2048,128]{1,0:T(8,128)(2,1)S(1)}, u32[]{:S(2)}, u32[]{:S(2)}) collective-permute-start(bf16[2048,128]{1,0:T(8,128)(2,1)S(1)} %join.1.refs_1_), channel_id=1, source_target_pairs={{0,16},{16,0},{32,48},{48,32},{64,80},{80,64},{96,112},{112,96},{1... | collective-permute-start | bytes 1572872 | tf_op jit(solution)/shard_map/ppermute | solution.py:396
  42.6 10.7 %collective-permute-start.16 = (bf16[8,128,128]{2,1,0:T(8,128)(2,1)S(1)}, bf16[8,128,128]{2,1,0:T(8,128)(2,1)S(1)}, u32[]{:S(2)}, u32[]{:S(2)}) collective-permute-start(bf16[8,128,128]{2,1,0:T(8,128)(2,1)S(1)} %get-tuple-element.60), channel_id=1, source_target_pairs={{0,1},{1,0},{2,3},{3,2},{4,5},{5,4},{6,7},{7,6},{8,9},{9,8},{10,11... | collective-permute-start | bytes 786440 | tf_op jit(solution)/shard_map/ppermute | solution.py:436
  45.0 19.2 %collective-permute-start.15 = (bf16[16,128,128]{2,1,0:T(8,128)(2,1)S(1)}, bf16[16,128,128]{2,1,0:T(8,128)(2,1)S(1)}, u32[]{:S(2)}, u32[]{:S(2)}) collective-permute-start(bf16[16,128,128]{2,1,0:T(8,128)(2,1)S(1)} %get-tuple-element.59), channel_id=1, source_target_pairs={{0,1},{1,0},{2,3},{3,2},{4,5},{5,4},{6,7},{7,6},{8,9},{9,8},{10,11... | collective-permute-start | bytes 1572872 | tf_op jit(solution)/shard_map/ppermute | solution.py:436
  53.5 12.4 %collective-permute-start.17 = (bf16[8,128,128]{2,1,0:T(8,128)(2,1)S(1)}, bf16[8,128,128]{2,1,0:T(8,128)(2,1)S(1)}, u32[]{:S(2)}, u32[]{:S(2)}) collective-permute-start(bf16[8,128,128]{2,1,0:T(8,128)(2,1)S(1)} %get-tuple-element.61), channel_id=1, source_target_pairs={{0,2},{1,3},{2,4},{3,5},{4,6},{5,7},{6,8},{7,9},{8,10},{9,11},{10,... | collective-permute-start | bytes 786440 | tf_op jit(solution)/shard_map/ppermute | solution.py:446
  56.2 11.3 %collective-permute-start.21 = (bf16[8,128,128]{2,1,0:T(8,128)(2,1)S(1)}, bf16[8,128,128]{2,1,0:T(8,128)(2,1)S(1)}, u32[]{:S(2)}, u32[]{:S(2)}) collective-permute-start(bf16[8,128,128]{2,1,0:T(8,128)(2,1)S(1)} %get-tuple-element.62), channel_id=1, source_target_pairs={{0,14},{1,15},{2,0},{3,1},{4,2},{5,3},{6,4},{7,5},{8,6},{9,7},{10,... | collective-permute-start | bytes 786440 | tf_op jit(solution)/shard_map/ppermute | solution.py:446
  59.4 15.9 %collective-permute-start.14 = (bf16[16,128,128]{2,1,0:T(8,128)(2,1)S(1)}, bf16[16,128,128]{2,1,0:T(8,128)(2,1)S(1)}, u32[]{:S(2)}, u32[]{:S(2)}) collective-permute-start(bf16[16,128,128]{2,1,0:T(8,128)(2,1)S(1)} %get-tuple-element.58), channel_id=1, source_target_pairs={{0,1},{1,0},{2,3},{3,2},{4,5},{5,4},{6,7},{7,6},{8,9},{9,8},{10,11... | collective-permute-start | bytes 1572872 | tf_op jit(solution)/shard_map/ppermute | solution.py:436
  66.0 16.7 %collective-permute-start.18 = (bf16[16,128,128]{2,1,0:T(8,128)(2,1)S(1)}, bf16[16,128,128]{2,1,0:T(8,128)(2,1)S(1)}, u32[]{:S(2)}, u32[]{:S(2)}) collective-permute-start(bf16[16,128,128]{2,1,0:T(8,128)(2,1)S(1)} %hop_3.1), channel_id=1, source_target_pairs={{0,2},{1,3},{2,4},{3,5},{4,6},{5,7},{6,8},{7,9},{8,10},{9,11},{10,... | collective-permute-start | bytes 1572872 | tf_op jit(solution)/shard_map/ppermute | solution.py:446
  67.6 15.4 %collective-permute-start.22 = (bf16[16,128,128]{2,1,0:T(8,128)(2,1)S(1)}, bf16[16,128,128]{2,1,0:T(8,128)(2,1)S(1)}, u32[]{:S(2)}, u32[]{:S(2)}) collective-permute-start(bf16[16,128,128]{2,1,0:T(8,128)(2,1)S(1)} %hop_5.1), channel_id=1, source_target_pairs={{0,14},{1,15},{2,0},{3,1},{4,2},{5,3},{6,4},{7,5},{8,6},{9,7},{10,... | collective-permute-start | bytes 1572872 | tf_op jit(solution)/shard_map/ppermute | solution.py:446
  70.8 15.7 %collective-permute-start.13 = (bf16[16,128,128]{2,1,0:T(8,128)(2,1)S(1)}, bf16[16,128,128]{2,1,0:T(8,128)(2,1)S(1)}, u32[]{:S(2)}, u32[]{:S(2)}) collective-permute-start(bf16[16,128,128]{2,1,0:T(8,128)(2,1)S(1)} %get-tuple-element.57), channel_id=1, source_target_pairs={{0,1},{1,0},{2,3},{3,2},{4,5},{5,4},{6,7},{7,6},{8,9},{9,8},{10,11... | collective-permute-start | bytes 1572872 | tf_op jit(solution)/shard_map/ppermute | solution.py:436
  82.9 14.7 %collective-permute-start.19 = (bf16[16,128,128]{2,1,0:T(8,128)(2,1)S(1)}, bf16[16,128,128]{2,1,0:T(8,128)(2,1)S(1)}, u32[]{:S(2)}, u32[]{:S(2)}) collective-permute-start(bf16[16,128,128]{2,1,0:T(8,128)(2,1)S(1)} %hop_2.1), channel_id=1, source_target_pairs={{0,2},{1,3},{2,4},{3,5},{4,6},{5,7},{6,8},{7,9},{8,10},{9,11},{10,... | collective-permute-start | bytes 1572872 | tf_op jit(solution)/shard_map/ppermute | solution.py:446
  83.2 14.7 %collective-permute-start.23 = (bf16[16,128,128]{2,1,0:T(8,128)(2,1)S(1)}, bf16[16,128,128]{2,1,0:T(8,128)(2,1)S(1)}, u32[]{:S(2)}, u32[]{:S(2)}) collective-permute-start(bf16[16,128,128]{2,1,0:T(8,128)(2,1)S(1)} %hop_6.1), channel_id=1, source_target_pairs={{0,14},{1,15},{2,0},{3,1},{4,2},{5,3},{6,4},{7,5},{8,6},{9,7},{10,... | collective-permute-start | bytes 1572872 | tf_op jit(solution)/shard_map/ppermute | solution.py:446
  97.8 13.8 %copy-start.2 = (bf16[128,256]{1,0:T(8,128)(2,1)S(1)}, bf16[128,256]{1,0:T(8,128)(2,1)}, u32[]{:S(2)}) copy-start(bf16[128,256]{1,0:T(8,128)(2,1)} %weight.1) | copy-start | bytes 196612
  97.8 13.8 %copy-start.3 = (f32[256]{0:T(256)S(1)}, f32[256]{0:T(256)}, u32[]{:S(2)}) copy-start(f32[256]{0:T(256)} %param.13) | copy-start | bytes 3076
  97.8 13.8 %collective-permute-start.20 = (bf16[16,128,128]{2,1,0:T(8,128)(2,1)S(1)}, bf16[16,128,128]{2,1,0:T(8,128)(2,1)S(1)}, u32[]{:S(2)}, u32[]{:S(2)}) collective-permute-start(bf16[16,128,128]{2,1,0:T(8,128)(2,1)S(1)} %hop_1.1), channel_id=1, source_target_pairs={{0,2},{1,3},{2,4},{3,5},{4,6},{5,7},{6,8},{7,9},{8,10},{9,11},{10,... | collective-permute-start | bytes 1572872 | tf_op jit(solution)/shard_map/ppermute | solution.py:459
  98.1 13.5 %collective-permute-start.24 = (bf16[16,128,128]{2,1,0:T(8,128)(2,1)S(1)}, bf16[16,128,128]{2,1,0:T(8,128)(2,1)S(1)}, u32[]{:S(2)}, u32[]{:S(2)}) collective-permute-start(bf16[16,128,128]{2,1,0:T(8,128)(2,1)S(1)} %hop_7.1), channel_id=1, source_target_pairs={{0,14},{1,15},{2,0},{3,1},{4,2},{5,3},{6,4},{7,5},{8,6},{9,7},{10,... | collective-permute-start | bytes 1572872 | tf_op jit(solution)/shard_map/ppermute | solution.py:459
  101.4 7.9 %collective-permute-start.12 = (bf16[8,128,128]{2,1,0:T(8,128)(2,1)S(1)}, bf16[8,128,128]{2,1,0:T(8,128)(2,1)S(1)}, u32[]{:S(2)}, u32[]{:S(2)}) collective-permute-start(bf16[8,128,128]{2,1,0:T(8,128)(2,1)S(1)} %get-tuple-element.56), channel_id=1, source_target_pairs={{0,1},{1,0},{2,3},{3,2},{4,5},{5,4},{6,7},{7,6},{8,9},{9,8},{10,11... | collective-permute-start | bytes 786440 | tf_op jit(solution)/shard_map/ppermute | solution.py:436
where the time goes:
time: 115 us; the launch traced here: 113 us
  waiting for transfers between devices  55.3 us (48%)
  starting transfers between devices  37.5 us (33%)
  Pallas kernels  14.1 us (12%)
  local copies, waits for them, and re-layouts  4.66 us (4%)
    ppermute x8, waiting for transfers between devices, on_device(): chains = [lax.ppermute(c, 'col', p) for c, p in zip(chains, Z_CHAINS)]  22.5 us
    ppermute x8, starting transfers between devices, on_device(): chains = [lax.ppermute(c, 'col', p) for c, p in zip(chains, Z_CHAINS)]  17.3 us
    ppermute x5, waiting for transfers between devices, on_device(): part = lax.ppermute(part, 'col', X_FLIP)  16.3 us
    ppermute x11, waiting for transfers between devices, send(): return lax.ppermute(array, 'row', perm)  15.1 us
    ppermute x11, starting transfers between devices, send(): return lax.ppermute(array, 'row', perm)  9.32 us
    ppermute x5, starting transfers between devices, on_device(): part = lax.ppermute(part, 'col', X_FLIP)  8.48 us
    pallas_call x3, Pallas kernels, more_products(): call(functools.partial(more_kernel, kinds, len(feats)), name, out_shape=[...  4.6 us
    unnamed x10, local copies, waits for them, and re-layouts  4.54 us
  transfers between devices with their start and end apart: 25, of which 16 were waited for; matrix products, arithmetic and copies ran while one was open for 1% of the time, Pallas kernels for 10%

commit v1 on v0

--- a/solution.py
+++ b/solution.py
@@ -23,7 +23,7 @@
 PACKED = ((0, 0), (1, 0), (3, 0), (0, 1), (2, 0), (3, 1), (1, 1), (2, 1))
 EARLY = 4
 LAST = 7
-X_PARTS = ((4,), (3, 5), (2, 6), (1, 7), (0,))
+X_PARTS = ((4,), (3,), (5,), (2, 6), (1, 7), (0,))
 THIRDS = (752, 880, 416)
 
 VMEM = pltpu.VMEM
@@ -248,6 +248,28 @@
     )(*([keep(base)] if has_base else []), *arrays)
 
 
+def pack_second_kernel(_, up_side, down_side, far, packed, *thirds):
+    for i, ref in enumerate((far, down_side, up_side)):
+        packed[pl.ds((EARLY + i) * ROWS, ROWS), :] = ref[...]
+    at = 0
+    for n, ref, third in zip(THIRDS, (up_side, down_side, far), thirds):
+        third[...] = ref[pl.ds(at, n), :]
+        at += n
+
+
+def pack_second(base, arrays):
+    width = base.shape[1]
+    packed, *thirds = call(
+        pack_second_kernel,
+        "pack_second",
+        out_shape=[VMEM(base.shape, base.dtype)] + [VMEM((n, width), base.dtype) for n in THIRDS],
+        in_specs=[VMEM_SPEC] * 4,
+        out_specs=[VMEM_SPEC] * 4,
+        input_output_aliases={0: 0},
+    )(keep(base), *arrays)
+    return packed, thirds
+
+
 def join_kernel(*refs):
     at = 0
     for ref in refs[:-1]:
@@ -414,13 +436,8 @@
         (far, down_side, up_side, feats, other, own)
     )
     partner_dest = lax.ppermute(dest, "col", X_FLIP)
-    thirds, at = [], 0
-    for n, array, perm in zip(
-        THIRDS, (up_side, down_side, far), (FROM_UP, FROM_DOWN, FROM_SIDE)
-    ):
-        thirds.append(send(array[at : at + n], perm))
-        at += n
-    feats = pack(feats, EARLY * ROWS, [far, down_side, up_side])
+    feats, parts = pack_second(feats, (up_side, down_side, far))
+    thirds = [send(p, perm) for p, perm in zip(parts, (FROM_UP, FROM_DOWN, FROM_SIDE))]
     sibling = send(feats, FROM_CORE)
     kinds = (((1, 0),), ((CLASSES + 1, 0),))
     other, own = more_products("late_products", kinds, plan, tiles, [feats], [other, own])

time: 115 us -> 111 us (0.965)
  the two profiles are of different devices: /device:TPU:26 before, /device:TPU:1 now
where the time goes in v1:
time: 111 us; the launch traced here: 109 us
  starting transfers between devices  49.2 us (44%)
  waiting for transfers between devices  37.9 us (34%)
  Pallas kernels  15.9 us (14%)
  local copies, waits for them, and re-layouts  4.62 us (4%)
    ppermute x8, starting transfers between devices, on_device(): chains = [lax.ppermute(c, 'col', p) for c, p in zip(chains, Z_CHAINS)]  18.4 us
    ppermute x11, starting transfers between devices, send(): return lax.ppermute(array, 'row', perm)  18.2 us
    ppermute x8, waiting for transfers between devices, on_device(): chains = [lax.ppermute(c, 'col', p) for c, p in zip(chains, Z_CHAINS)]  17.6 us
    ppermute x6, waiting for transfers between devices, on_device(): part = lax.ppermute(part, 'col', X_FLIP)  11.2 us
    ppermute x6, starting transfers between devices, on_device(): part = lax.ppermute(part, 'col', X_FLIP)  9.32 us
    ppermute x11, waiting for transfers between devices, send(): return lax.ppermute(array, 'row', perm)  8.47 us
    pallas_call x3, Pallas kernels, more_products(): call(functools.partial(more_kernel, kinds, len(feats)), name, out_shape=[...  6.11 us
    unnamed x10, local copies, waits for them, and re-layouts  4.54 us
  transfers between devices with their start and end apart: 26, of which 19 were waited for; matrix products, arithmetic and copies ran while one was open for 1% of the time, Pallas kernels for 12%

profile of v1, /device:TPU:1, one launch (start us, length us, event | category | flops | bytes accessed | tf_op | source)
XLA Modules:
  0.0 109.2 jit_solution(990449902455962876)
XLA Ops:
  0.0 2.1 %collective-permute-start.1 = (bf16[2048,128]{1,0:T(8,128)(2,1)}, bf16[2048,128]{1,0:T(8,128)(2,1)S(1)}, u32[]{:S(2)}, u32[]{:S(2)}) collective-permute-start(bf16[2048,128]{1,0:T(8,128)(2,1)} %refs_0_.1), channel_id=1, source_target_pairs={{0,64},{16,80},{32,96},{48,112},{64,128},{80,144},{96,160},{112,17... | collective-permute-start | bytes 1572872 | tf_op jit(solution)/shard_map/ppermute | solution.py:418
  2.1 1.4 %collective-permute-start = (bf16[2048,128]{1,0:T(8,128)(2,1)}, bf16[2048,128]{1,0:T(8,128)(2,1)S(1)}, u32[]{:S(2)}, u32[]{:S(2)}) collective-permute-start(bf16[2048,128]{1,0:T(8,128)(2,1)} %refs_0_.1), channel_id=1, source_target_pairs={{0,192},{16,208},{32,224},{48,240},{64,0},{80,16},{96,32},{112,48}... | collective-permute-start | bytes 1572872 | tf_op jit(solution)/shard_map/ppermute | solution.py:418
  3.6 1.2 %collective-permute-start.2 = (bf16[2048,128]{1,0:T(8,128)(2,1)}, bf16[2048,128]{1,0:T(8,128)(2,1)S(1)}, u32[]{:S(2)}, u32[]{:S(2)}) collective-permute-start(bf16[2048,128]{1,0:T(8,128)(2,1)} %refs_0_.1), channel_id=1, source_target_pairs={{0,32},{16,48},{32,0},{48,16},{64,96},{80,112},{96,64},{112,80},{1... | collective-permute-start | bytes 1572872 | tf_op jit(solution)/shard_map/ppermute | solution.py:418
  5.5 0.7 compare_select_fusion.dest
  6.2 0.7 copy-done.4
  6.9 1.0 plan.1
  7.9 5.5 %collective-permute-done.1.refs_2_ = bf16[2048,128]{1,0:T(8,128)(2,1)S(1)} collective-permute-done((bf16[2048,128]{1,0:T(8,128)(2,1)}, bf16[2048,128]{1,0:T(8,128)(2,1)S(1)}, u32[]{:S(2)}, u32[]{:S(2)}) %collective-permute-start.1) | collective-permute-done | bytes 524320 | tf_op jit(solution)/shard_map/ppermute | solution.py:418
  13.4 1.3 %collective-permute-done.refs_1_ = bf16[2048,128]{1,0:T(8,128)(2,1)S(1)} collective-permute-done((bf16[2048,128]{1,0:T(8,128)(2,1)}, bf16[2048,128]{1,0:T(8,128)(2,1)S(1)}, u32[]{:S(2)}, u32[]{:S(2)}) %collective-permute-start) | collective-permute-done | bytes 524320 | tf_op jit(solution)/shard_map/ppermute | solution.py:418
  14.6 0.2 collective-permute-done.2.refs_3_
  14.9 1.3 %collective-permute-start.4 = (bf16[2048,128]{1,0:T(8,128)(2,1)S(1)}, bf16[2048,128]{1,0:T(8,128)(2,1)S(1)}, u32[]{:S(2)}, u32[]{:S(2)}) collective-permute-start(bf16[2048,128]{1,0:T(8,128)(2,1)S(1)} %collective-permute-done.2.refs_3_), channel_id=1, source_target_pairs={{0,64},{16,80},{32,96},{48,112},{64,128},{80,144},{96,160},{112,17... | collective-permute-start | bytes 1572872 | tf_op jit(solution)/shard_map/ppermute | solution.py:418
  16.1 1.2 %collective-permute-start.5 = (bf16[2048,128]{1,0:T(8,128)(2,1)S(1)}, bf16[2048,128]{1,0:T(8,128)(2,1)S(1)}, u32[]{:S(2)}, u32[]{:S(2)}) collective-permute-start(bf16[2048,128]{1,0:T(8,128)(2,1)S(1)} %collective-permute-done.refs_1_), channel_id=1, source_target_pairs={{0,32},{16,48},{32,0},{48,16},{64,96},{80,112},{96,64},{112,80},{1... | collective-permute-start | bytes 1572872 | tf_op jit(solution)/shard_map/ppermute | solution.py:418
  17.3 2.3 %collective-permute-start.3 = (bf16[2048,128]{1,0:T(8,128)(2,1)S(1)}, bf16[2048,128]{1,0:T(8,128)(2,1)S(1)}, u32[]{:S(2)}, u32[]{:S(2)}) collective-permute-start(bf16[2048,128]{1,0:T(8,128)(2,1)S(1)} %collective-permute-done.refs_1_), channel_id=1, source_target_pairs={{0,192},{16,208},{32,224},{48,240},{64,0},{80,16},{96,32},{112,48}... | collective-permute-start | bytes 1572872 | tf_op jit(solution)/shard_map/ppermute | solution.py:418
  19.6 3.4 %copy-done = bf16[1,1,256,128,128]{4,3,2,1,0:T(8,128)(2,1)S(1)} copy-done((bf16[1,1,256,128,128]{4,3,2,1,0:T(8,128)(2,1)S(1)}, bf16[1,1,256,128,128]{4,3,2,1,0:T(8,128)(2,1)}, u32[]{:S(2)}) %copy-start) | copy-done | bytes 8388632
  23.0 0.6 load_tiles.1.tiles
  23.6 0.5 copy-done.1
  24.1 0.1 pack.1.feats
  24.2 2.6 %first_products.1 = (bf16[14336,128]{1,0:T(8,128)(2,1)S(1)}, f32[65,128,128]{2,1,0:T(8,128)S(1)}, f32[129,128,128]{2,1,0:T(8,128)S(1)}) custom-call(s32[8,512]{1,0:T(8,128)S(1)} %plan.1, bf16[256,128,128]{2,1,0:T(8,128)(2,1)S(1)} %load_tiles.1.tiles, bf16[14336,128]{1,0:T(8,128)(2,1)S(1)} %pack.1.feats), custom_call_target="tpu_custom_call", output_to_operand_aliasing={{0}: (2, {})} | custom-call | tf_op jit(solution)/shard_map/first_products/pallas_call | solution.py:299
  26.8 0.4 collective-permute-done.5.up_side
  27.2 0.9 collective-permute-done.3.far
  28.1 0.1 pack_second.1
  28.3 3.7 %collective-permute-start.10 = (bf16[14336,128]{1,0:T(8,128)(2,1)S(1)}, bf16[14336,128]{1,0:T(8,128)(2,1)S(1)}, u32[]{:S(2)}, u32[]{:S(2)}) collective-permute-start(bf16[14336,128]{1,0:T(8,128)(2,1)S(1)} %get-tuple-element.53.refs_0_), channel_id=1, source_target_pairs={{0,16},{16,0},{32,48},{48,32},{64,80},{80,64},{96,112},{112,96},{1... | collective-permute-start | bytes 11010056 | tf_op jit(solution)/shard_map/ppermute | solution.py:418
  32.0 1.1 collective-permute-start.7
  33.1 2.3 %collective-permute-start.6 = (bf16[752,128]{1,0:T(8,128)(2,1)S(1)}, bf16[752,128]{1,0:T(8,128)(2,1)S(1)}, u32[]{:S(2)}, u32[]{:S(2)}) collective-permute-start(bf16[752,128]{1,0:T(8,128)(2,1)S(1)} %get-tuple-element.50), channel_id=1, source_target_pairs={{0,192},{16,208},{32,224},{48,240},{64,0},{80,16},{96,32},{112,48}... | collective-permute-start | bytes 577544 | tf_op jit(solution)/shard_map/ppermute | solution.py:418
  35.4 3.3 %collective-permute-start.9 = (s32[1,256]{1,0:T(1,128)S(1)}, s32[1,256]{1,0:T(1,128)S(1)}, u32[]{:S(2)}, u32[]{:S(2)}) collective-permute-start(s32[1,256]{1,0:T(1,128)S(1)} %compare_select_fusion.dest), channel_id=1, source_target_pairs={{0,1},{1,0},{2,3},{3,2},{4,5},{5,4},{6,7},{7,6},{8,9},{9,8},{10,11... | collective-permute-start | bytes 3080 | tf_op jit(solution)/shard_map/ppermute | solution.py:438
  38.7 1.7 %late_products.1 = (f32[65,128,128]{2,1,0:T(8,128)S(1)}, f32[129,128,128]{2,1,0:T(8,128)S(1)}) custom-call(s32[8,512]{1,0:T(8,128)S(1)} %plan.1, bf16[256,128,128]{2,1,0:T(8,128)(2,1)S(1)} %load_tiles.1.tiles, bf16[14336,128]{1,0:T(8,128)(2,1)S(1)} %get-tuple-element.53.refs_0_, ...), custom_call_target="tpu_custom_call", output_to_operand_aliasing={{0}: (3, {}), {1}: (4, {})} | custom-call | tf_op jit(solution)/shard_map/late_products/pallas_call | solution.py:322
  40.4 0.6 collective-permute-done.9.partner_dest
  41.0 0.2 collective-permute-done.7.refs_1_
  41.2 1.5 %collective-permute-start.11 = (bf16[2048,128]{1,0:T(8,128)(2,1)S(1)}, bf16[2048,128]{1,0:T(8,128)(2,1)S(1)}, u32[]{:S(2)}, u32[]{:S(2)}) collective-permute-start(bf16[2048,128]{1,0:T(8,128)(2,1)S(1)} %join.1.refs_1_), channel_id=1, source_target_pairs={{0,16},{16,0},{32,48},{48,32},{64,80},{80,64},{96,112},{112,96},{1... | collective-permute-start | bytes 1572872 | tf_op jit(solution)/shard_map/ppermute | solution.py:418
  42.8 2.0 %other_half.1._ = f32[65,128,128]{2,1,0:T(8,128)S(1)} custom-call(s32[8,512]{1,0:T(8,128)S(1)} %plan.1, bf16[256,128,128]{2,1,0:T(8,128)(2,1)S(1)} %load_tiles.1.tiles, bf16[14336,128]{1,0:T(8,128)(2,1)S(1)} %collective-permute-done.10.refs_0_, bf16[2048,128]{1,0:T(8,128)(2,1)S(1)} %join.1.refs_1_, ...), custom_call_target="tpu_custom_call", output_to_operand_aliasing={{}: (4, {})} | custom-call | tf_op jit(solution)/shard_map/other_half/pallas_call | solution.py:322
  44.8 1.1 %first_send.1 = (f32[65,128,128]{2,1,0:T(8,128)S(1)}, bf16[8,128,128]{2,1,0:T(8,128)(2,1)S(1)}) custom-call(s32[8,512]{1,0:T(8,128)S(1)} %plan.1, bf16[256,128,128]{2,1,0:T(8,128)(2,1)S(1)} %load_tiles.1.tiles, bf16[2048,128]{1,0:T(8,128)(2,1)S(1)} %collective-permute-done.11.refs_2_.far_sibling, ...), custom_call_target="tpu_custom_call", output_to_operand_aliasing={{0}: (3, {})} | custom-call | tf_op jit(solution)/shard_map/first_send/pallas_call | solution.py:350
  46.0 2.1 %collective-permute-start.16 = (bf16[8,128,128]{2,1,0:T(8,128)(2,1)S(1)}, bf16[8,128,128]{2,1,0:T(8,128)(2,1)S(1)}, u32[]{:S(2)}, u32[]{:S(2)}) collective-permute-start(bf16[8,128,128]{2,1,0:T(8,128)(2,1)S(1)} %get-tuple-element.69), channel_id=1, source_target_pairs={{0,1},{1,0},{2,3},{3,2},{4,5},{5,4},{6,7},{7,6},{8,9},{9,8},{10,11... | collective-permute-start | bytes 786440 | tf_op jit(solution)/shard_map/ppermute | solution.py:453
  48.0 1.3 %partner_map.1.slots = s32[1,128]{1,0:T(1,128)S(4)} custom-call(s32[5]{0:T(128)S(1)} %stack.23.where, s32[1,256]{1,0:T(1,128)S(1)} %collective-permute-done.9.partner_dest), custom_call_target="tpu_custom_call" | custom-call | tf_op jit(solution)/shard_map/partner_map/pallas_call | solution.py:179
  49.3 0.2 other_sends.1
  49.5 1.3 %collective-permute-start.15 = (bf16[8,128,128]{2,1,0:T(8,128)(2,1)S(1)}, bf16[8,128,128]{2,1,0:T(8,128)(2,1)S(1)}, u32[]{:S(2)}, u32[]{:S(2)}) collective-permute-start(bf16[8,128,128]{2,1,0:T(8,128)(2,1)S(1)} %get-tuple-element.68), channel_id=1, source_target_pairs={{0,1},{1,0},{2,3},{3,2},{4,5},{5,4},{6,7},{7,6},{8,9},{9,8},{10,11... | collective-permute-start | bytes 786440 | tf_op jit(solution)/shard_map/ppermute | solution.py:453
  50.8 2.3 %own_half.1.own = f32[129,128,128]{2,1,0:T(8,128)S(1)} custom-call(s32[8,512]{1,0:T(8,128)S(1)} %plan.1, bf16[256,128,128]{2,1,0:T(8,128)(2,1)S(1)} %load_tiles.1.tiles, bf16[14336,128]{1,0:T(8,128)(2,1)S(1)} %collective-permute-done.10.refs_0_, bf16[2048,128]{1,0:T(8,128)(2,1)S(1)} %join.1.refs_1_, ...), custom_call_target="tpu_custom_call", output_to_operand_aliasing={{}: (5, {})} | custom-call | tf_op jit(solution)/shard_map/own_half/pallas_call | solution.py:322
  53.2 2.4 %collective-permute-done.16.arrived = bf16[8,128,128]{2,1,0:T(8,128)(2,1)S(1)} collective-permute-done((bf16[8,128,128]{2,1,0:T(8,128)(2,1)S(1)}, bf16[8,128,128]{2,1,0:T(8,128)(2,1)S(1)}, u32[]{:S(2)}, u32[]{:S(2)}) %collective-permute-start.16) | collective-permute-done | bytes 262176 | tf_op jit(solution)/shard_map/ppermute | solution.py:453
  55.6 0.1 hop_4.1
  55.7 1.7 %collective-permute-start.17 = (bf16[8,128,128]{2,1,0:T(8,128)(2,1)S(1)}, bf16[8,128,128]{2,1,0:T(8,128)(2,1)S(1)}, u32[]{:S(2)}, u32[]{:S(2)}) collective-permute-start(bf16[8,128,128]{2,1,0:T(8,128)(2,1)S(1)} %get-tuple-element.70), channel_id=1, source_target_pairs={{0,2},{1,3},{2,4},{3,5},{4,6},{5,7},{6,8},{7,9},{8,10},{9,11},{10,... | collective-permute-start | bytes 786440 | tf_op jit(solution)/shard_map/ppermute | solution.py:463
  57.4 1.4 %collective-permute-start.21 = (bf16[8,128,128]{2,1,0:T(8,128)(2,1)S(1)}, bf16[8,128,128]{2,1,0:T(8,128)(2,1)S(1)}, u32[]{:S(2)}, u32[]{:S(2)}) collective-permute-start(bf16[8,128,128]{2,1,0:T(8,128)(2,1)S(1)} %get-tuple-element.71), channel_id=1, source_target_pairs={{0,1},{1,0},{2,3},{3,2},{4,5},{5,4},{6,7},{7,6},{8,9},{9,8},{10,11... | collective-permute-start | bytes 786440 | tf_op jit(solution)/shard_map/ppermute | solution.py:453
  58.8 4.5 %collective-permute-start.22 = (bf16[8,128,128]{2,1,0:T(8,128)(2,1)S(1)}, bf16[8,128,128]{2,1,0:T(8,128)(2,1)S(1)}, u32[]{:S(2)}, u32[]{:S(2)}) collective-permute-start(bf16[8,128,128]{2,1,0:T(8,128)(2,1)S(1)} %get-tuple-element.72), channel_id=1, source_target_pairs={{0,14},{1,15},{2,0},{3,1},{4,2},{5,3},{6,4},{7,5},{8,6},{9,7},{10,... | collective-permute-start | bytes 786440 | tf_op jit(solution)/shard_map/ppermute | solution.py:463
  63.3 1.1 collective-permute-start.14
  64.4 2.5 %collective-permute-done.17.refs_0_ = bf16[8,128,128]{2,1,0:T(8,128)(2,1)S(1)} collective-permute-done((bf16[8,128,128]{2,1,0:T(8,128)(2,1)S(1)}, bf16[8,128,128]{2,1,0:T(8,128)(2,1)S(1)}, u32[]{:S(2)}, u32[]{:S(2)}) %collective-permute-start.17) | collective-permute-done | bytes 262176 | tf_op jit(solution)/shard_map/ppermute | solution.py:463
  66.9 0.2 hop_3.1
  67.2 0.2 collective-permute-done.22.refs_0_
  67.5 0.2 hop_5.1
  67.6 5.0 %collective-permute-start.23 = (bf16[16,128,128]{2,1,0:T(8,128)(2,1)S(1)}, bf16[16,128,128]{2,1,0:T(8,128)(2,1)S(1)}, u32[]{:S(2)}, u32[]{:S(2)}) collective-permute-start(bf16[16,128,128]{2,1,0:T(8,128)(2,1)S(1)} %hop_5.1), channel_id=1, source_target_pairs={{0,14},{1,15},{2,0},{3,1},{4,2},{5,3},{6,4},{7,5},{8,6},{9,7},{10,... | collective-permute-start | bytes 1572872 | tf_op jit(solution)/shard_map/ppermute | solution.py:463
  72.6 1.9 %collective-permute-start.13 = (bf16[16,128,128]{2,1,0:T(8,128)(2,1)S(1)}, bf16[16,128,128]{2,1,0:T(8,128)(2,1)S(1)}, u32[]{:S(2)}, u32[]{:S(2)}) collective-permute-start(bf16[16,128,128]{2,1,0:T(8,128)(2,1)S(1)} %get-tuple-element.66), channel_id=1, source_target_pairs={{0,1},{1,0},{2,3},{3,2},{4,5},{5,4},{6,7},{7,6},{8,9},{9,8},{10,11... | collective-permute-start | bytes 1572872 | tf_op jit(solution)/shard_map/ppermute | solution.py:453
  74.5 2.0 %collective-permute-done.14.arrived = bf16[16,128,128]{2,1,0:T(8,128)(2,1)S(1)} collective-permute-done((bf16[16,128,128]{2,1,0:T(8,128)(2,1)S(1)}, bf16[16,128,128]{2,1,0:T(8,128)(2,1)S(1)}, u32[]{:S(2)}, u32[]{:S(2)}) %collective-permute-start.14) | collective-permute-done | bytes 524320 | tf_op jit(solution)/shard_map/ppermute | solution.py:453
  76.5 3.7 %collective-permute-done.18.refs_0_ = bf16[16,128,128]{2,1,0:T(8,128)(2,1)S(1)} collective-permute-done((bf16[16,128,128]{2,1,0:T(8,128)(2,1)S(1)}, bf16[16,128,128]{2,1,0:T(8,128)(2,1)S(1)}, u32[]{:S(2)}, u32[]{:S(2)}) %collective-permute-start.18) | collective-permute-done | bytes 524320 | tf_op jit(solution)/shard_map/ppermute | solution.py:463
  80.2 0.2 hop_2.1
  80.5 2.3 %collective-permute-done.23.refs_0_ = bf16[16,128,128]{2,1,0:T(8,128)(2,1)S(1)} collective-permute-done((bf16[16,128,128]{2,1,0:T(8,128)(2,1)S(1)}, bf16[16,128,128]{2,1,0:T(8,128)(2,1)S(1)}, u32[]{:S(2)}, u32[]{:S(2)}) %collective-permute-start.23) | collective-permute-done | bytes 524320 | tf_op jit(solution)/shard_map/ppermute | solution.py:463
  82.8 0.2 hop_6.1
  83.0 3.5 %collective-permute-start.24 = (bf16[16,128,128]{2,1,0:T(8,128)(2,1)S(1)}, bf16[16,128,128]{2,1,0:T(8,128)(2,1)S(1)}, u32[]{:S(2)}, u32[]{:S(2)}) collective-permute-start(bf16[16,128,128]{2,1,0:T(8,128)(2,1)S(1)} %hop_6.1), channel_id=1, source_target_pairs={{0,14},{1,15},{2,0},{3,1},{4,2},{5,3},{6,4},{7,5},{8,6},{9,7},{10,... | collective-permute-start | bytes 1572872 | tf_op jit(solution)/shard_map/ppermute | solution.py:463
  86.5 1.7 %collective-permute-done.13.arrived = bf16[16,128,128]{2,1,0:T(8,128)(2,1)S(1)} collective-permute-done((bf16[16,128,128]{2,1,0:T(8,128)(2,1)S(1)}, bf16[16,128,128]{2,1,0:T(8,128)(2,1)S(1)}, u32[]{:S(2)}, u32[]{:S(2)}) %collective-permute-start.13) | collective-permute-done | bytes 524320 | tf_op jit(solution)/shard_map/ppermute | solution.py:453
  88.1 5.9 %collective-permute-done.19.refs_0_ = bf16[16,128,128]{2,1,0:T(8,128)(2,1)S(1)} collective-permute-done((bf16[16,128,128]{2,1,0:T(8,128)(2,1)S(1)}, bf16[16,128,128]{2,1,0:T(8,128)(2,1)S(1)}, u32[]{:S(2)}, u32[]{:S(2)}) %collective-permute-start.19) | collective-permute-done | bytes 524320 | tf_op jit(solution)/shard_map/ppermute | solution.py:463
  94.0 0.2 hop_1.1
  94.3 1.4 %collective-permute-done.24.refs_0_ = bf16[16,128,128]{2,1,0:T(8,128)(2,1)S(1)} collective-permute-done((bf16[16,128,128]{2,1,0:T(8,128)(2,1)S(1)}, bf16[16,128,128]{2,1,0:T(8,128)(2,1)S(1)}, u32[]{:S(2)}, u32[]{:S(2)}) %collective-permute-start.24) | collective-permute-done | bytes 524320 | tf_op jit(solution)/shard_map/ppermute | solution.py:463
  95.7 0.2 hop_7.1
  95.9 3.5 %collective-permute-start.25 = (bf16[16,128,128]{2,1,0:T(8,128)(2,1)S(1)}, bf16[16,128,128]{2,1,0:T(8,128)(2,1)S(1)}, u32[]{:S(2)}, u32[]{:S(2)}) collective-permute-start(bf16[16,128,128]{2,1,0:T(8,128)(2,1)S(1)} %hop_7.1), channel_id=1, source_target_pairs={{0,14},{1,15},{2,0},{3,1},{4,2},{5,3},{6,4},{7,5},{8,6},{9,7},{10,... | collective-permute-start | bytes 1572872 | tf_op jit(solution)/shard_map/ppermute | solution.py:476
  99.4 1.6 %collective-permute-start.12 = (bf16[8,128,128]{2,1,0:T(8,128)(2,1)S(1)}, bf16[8,128,128]{2,1,0:T(8,128)(2,1)S(1)}, u32[]{:S(2)}, u32[]{:S(2)}) collective-permute-start(bf16[8,128,128]{2,1,0:T(8,128)(2,1)S(1)} %get-tuple-element.65), channel_id=1, source_target_pairs={{0,1},{1,0},{2,3},{3,2},{4,5},{5,4},{6,7},{7,6},{8,9},{9,8},{10,11... | collective-permute-start | bytes 786440 | tf_op jit(solution)/shard_map/ppermute | solution.py:453
  101.0 5.1 %collective-permute-done.12.arrived = bf16[8,128,128]{2,1,0:T(8,128)(2,1)S(1)} collective-permute-done((bf16[8,128,128]{2,1,0:T(8,128)(2,1)S(1)}, bf16[8,128,128]{2,1,0:T(8,128)(2,1)S(1)}, u32[]{:S(2)}, u32[]{:S(2)}) %collective-permute-start.12) | collective-permute-done | bytes 262176 | tf_op jit(solution)/shard_map/ppermute | solution.py:453
  106.1 0.1 collective-permute-done.20.passed_a
  106.2 1.5 %collective-permute-done.25.passed_b = bf16[16,128,128]{2,1,0:T(8,128)(2,1)S(1)} collective-permute-done((bf16[16,128,128]{2,1,0:T(8,128)(2,1)S(1)}, bf16[16,128,128]{2,1,0:T(8,128)(2,1)S(1)}, u32[]{:S(2)}, u32[]{:S(2)}) %collective-permute-start.25) | collective-permute-done | bytes 524320 | tf_op jit(solution)/shard_map/ppermute | solution.py:476
  107.7 1.5 %last.1 = bf16[2048,256]{1,0:T(8,128)(2,1)} custom-call(s32[1,128]{1,0:T(1,128)S(4)} %partner_map.1.slots, f32[129,128,128]{2,1,0:T(8,128)S(1)} %own_half.1.own, bf16[8,128,128]{2,1,0:T(8,128)(2,1)S(1)} %collective-permute-done.12.arrived, bf16[16,128,128]{2,1,0:T(8,128)(2,1)S(1)} %collective-permute-done.20.passed_a, ...), custom_call_target="tpu_custom_call" | custom-call | tf_op jit(solution)/shard_map/last/pallas_call | solution.py:408
  (20 shorter events, 0.4 us)
Async XLA Ops:
  0.0 13.4 %collective-permute-start.1 = (bf16[2048,128]{1,0:T(8,128)(2,1)}, bf16[2048,128]{1,0:T(8,128)(2,1)S(1)}, u32[]{:S(2)}, u32[]{:S(2)}) collective-permute-start(bf16[2048,128]{1,0:T(8,128)(2,1)} %refs_0_.1), channel_id=1, source_target_pairs={{0,64},{16,80},{32,96},{48,112},{64,128},{80,144},{96,160},{112,17... | collective-permute-start | bytes 1572872 | tf_op jit(solution)/shard_map/ppermute | solution.py:418
  2.1 12.5 %collective-permute-start = (bf16[2048,128]{1,0:T(8,128)(2,1)}, bf16[2048,128]{1,0:T(8,128)(2,1)S(1)}, u32[]{:S(2)}, u32[]{:S(2)}) collective-permute-start(bf16[2048,128]{1,0:T(8,128)(2,1)} %refs_0_.1), channel_id=1, source_target_pairs={{0,192},{16,208},{32,224},{48,240},{64,0},{80,16},{96,32},{112,48}... | collective-permute-start | bytes 1572872 | tf_op jit(solution)/shard_map/ppermute | solution.py:418
  3.6 11.3 %collective-permute-start.2 = (bf16[2048,128]{1,0:T(8,128)(2,1)}, bf16[2048,128]{1,0:T(8,128)(2,1)S(1)}, u32[]{:S(2)}, u32[]{:S(2)}) collective-permute-start(bf16[2048,128]{1,0:T(8,128)(2,1)} %refs_0_.1), channel_id=1, source_target_pairs={{0,32},{16,48},{32,0},{48,16},{64,96},{80,112},{96,64},{112,80},{1... | collective-permute-start | bytes 1572872 | tf_op jit(solution)/shard_map/ppermute | solution.py:418
  6.2 0.7 copy-start.4
  14.9 12.0 %collective-permute-start.4 = (bf16[2048,128]{1,0:T(8,128)(2,1)S(1)}, bf16[2048,128]{1,0:T(8,128)(2,1)S(1)}, u32[]{:S(2)}, u32[]{:S(2)}) collective-permute-start(bf16[2048,128]{1,0:T(8,128)(2,1)S(1)} %collective-permute-done.2.refs_3_), channel_id=1, source_target_pairs={{0,64},{16,80},{32,96},{48,112},{64,128},{80,144},{96,160},{112,17... | collective-permute-start | bytes 1572872 | tf_op jit(solution)/shard_map/ppermute | solution.py:418
  16.1 11.1 %collective-permute-start.5 = (bf16[2048,128]{1,0:T(8,128)(2,1)S(1)}, bf16[2048,128]{1,0:T(8,128)(2,1)S(1)}, u32[]{:S(2)}, u32[]{:S(2)}) collective-permute-start(bf16[2048,128]{1,0:T(8,128)(2,1)S(1)} %collective-permute-done.refs_1_), channel_id=1, source_target_pairs={{0,32},{16,48},{32,0},{48,16},{64,96},{80,112},{96,64},{112,80},{1... | collective-permute-start | bytes 1572872 | tf_op jit(solution)/shard_map/ppermute | solution.py:418
  17.3 10.8 %collective-permute-start.3 = (bf16[2048,128]{1,0:T(8,128)(2,1)S(1)}, bf16[2048,128]{1,0:T(8,128)(2,1)S(1)}, u32[]{:S(2)}, u32[]{:S(2)}) collective-permute-start(bf16[2048,128]{1,0:T(8,128)(2,1)S(1)} %collective-permute-done.refs_1_), channel_id=1, source_target_pairs={{0,192},{16,208},{32,224},{48,240},{64,0},{80,16},{96,32},{112,48}... | collective-permute-start | bytes 1572872 | tf_op jit(solution)/shard_map/ppermute | solution.py:418
  19.6 3.4 %copy-start = (bf16[1,1,256,128,128]{4,3,2,1,0:T(8,128)(2,1)S(1)}, bf16[1,1,256,128,128]{4,3,2,1,0:T(8,128)(2,1)}, u32[]{:S(2)}) copy-start(bf16[1,1,256,128,128]{4,3,2,1,0:T(8,128)(2,1)} %param.8) | copy-start | bytes 25165828
  23.0 1.0 copy-start.1
  28.3 14.5 %collective-permute-start.10 = (bf16[14336,128]{1,0:T(8,128)(2,1)S(1)}, bf16[14336,128]{1,0:T(8,128)(2,1)S(1)}, u32[]{:S(2)}, u32[]{:S(2)}) collective-permute-start(bf16[14336,128]{1,0:T(8,128)(2,1)S(1)} %get-tuple-element.53.refs_0_), channel_id=1, source_target_pairs={{0,16},{16,0},{32,48},{48,32},{64,80},{80,64},{96,112},{112,96},{1... | collective-permute-start | bytes 11010056 | tf_op jit(solution)/shard_map/ppermute | solution.py:418
  32.0 9.2 %collective-permute-start.7 = (bf16[880,128]{1,0:T(8,128)(2,1)S(1)}, bf16[880,128]{1,0:T(8,128)(2,1)S(1)}, u32[]{:S(2)}, u32[]{:S(2)}) collective-permute-start(bf16[880,128]{1,0:T(8,128)(2,1)S(1)} %get-tuple-element.51), channel_id=1, source_target_pairs={{0,64},{16,80},{32,96},{48,112},{64,128},{80,144},{96,160},{112,17... | collective-permute-start | bytes 675848 | tf_op jit(solution)/shard_map/ppermute | solution.py:418
  33.1 8.0 %collective-permute-start.6 = (bf16[752,128]{1,0:T(8,128)(2,1)S(1)}, bf16[752,128]{1,0:T(8,128)(2,1)S(1)}, u32[]{:S(2)}, u32[]{:S(2)}) collective-permute-start(bf16[752,128]{1,0:T(8,128)(2,1)S(1)} %get-tuple-element.50), channel_id=1, source_target_pairs={{0,192},{16,208},{32,224},{48,240},{64,0},{80,16},{96,32},{112,48}... | collective-permute-start | bytes 577544 | tf_op jit(solution)/shard_map/ppermute | solution.py:418
  35.4 5.6 %collective-permute-start.8 = (bf16[416,128]{1,0:T(8,128)(2,1)S(1)}, bf16[416,128]{1,0:T(8,128)(2,1)S(1)}, u32[]{:S(2)}, u32[]{:S(2)}) collective-permute-start(bf16[416,128]{1,0:T(8,128)(2,1)S(1)} %get-tuple-element.52), channel_id=1, source_target_pairs={{0,32},{16,48},{32,0},{48,16},{64,96},{80,112},{96,64},{112,80},{1... | collective-permute-start | bytes 319496 | tf_op jit(solution)/shard_map/ppermute | solution.py:418
  35.4 5.6 %collective-permute-start.9 = (s32[1,256]{1,0:T(1,128)S(1)}, s32[1,256]{1,0:T(1,128)S(1)}, u32[]{:S(2)}, u32[]{:S(2)}) collective-permute-start(s32[1,256]{1,0:T(1,128)S(1)} %compare_select_fusion.dest), channel_id=1, source_target_pairs={{0,1},{1,0},{2,3},{3,2},{4,5},{5,4},{6,7},{7,6},{8,9},{9,8},{10,11... | collective-permute-start | bytes 3080 | tf_op jit(solution)/shard_map/ppermute | solution.py:438
  41.2 3.6 %collective-permute-start.11 = (bf16[2048,128]{1,0:T(8,128)(2,1)S(1)}, bf16[2048,128]{1,0:T(8,128)(2,1)S(1)}, u32[]{:S(2)}, u32[]{:S(2)}) collective-permute-start(bf16[2048,128]{1,0:T(8,128)(2,1)S(1)} %join.1.refs_1_), channel_id=1, source_target_pairs={{0,16},{16,0},{32,48},{48,32},{64,80},{80,64},{96,112},{112,96},{1... | collective-permute-start | bytes 1572872 | tf_op jit(solution)/shard_map/ppermute | solution.py:418
  46.0 9.6 %collective-permute-start.16 = (bf16[8,128,128]{2,1,0:T(8,128)(2,1)S(1)}, bf16[8,128,128]{2,1,0:T(8,128)(2,1)S(1)}, u32[]{:S(2)}, u32[]{:S(2)}) collective-permute-start(bf16[8,128,128]{2,1,0:T(8,128)(2,1)S(1)} %get-tuple-element.69), channel_id=1, source_target_pairs={{0,1},{1,0},{2,3},{3,2},{4,5},{5,4},{6,7},{7,6},{8,9},{9,8},{10,11... | collective-permute-start | bytes 786440 | tf_op jit(solution)/shard_map/ppermute | solution.py:453
  49.5 14.9 %collective-permute-start.15 = (bf16[8,128,128]{2,1,0:T(8,128)(2,1)S(1)}, bf16[8,128,128]{2,1,0:T(8,128)(2,1)S(1)}, u32[]{:S(2)}, u32[]{:S(2)}) collective-permute-start(bf16[8,128,128]{2,1,0:T(8,128)(2,1)S(1)} %get-tuple-element.68), channel_id=1, source_target_pairs={{0,1},{1,0},{2,3},{3,2},{4,5},{5,4},{6,7},{7,6},{8,9},{9,8},{10,11... | collective-permute-start | bytes 786440 | tf_op jit(solution)/shard_map/ppermute | solution.py:453
  55.7 11.2 %collective-permute-start.17 = (bf16[8,128,128]{2,1,0:T(8,128)(2,1)S(1)}, bf16[8,128,128]{2,1,0:T(8,128)(2,1)S(1)}, u32[]{:S(2)}, u32[]{:S(2)}) collective-permute-start(bf16[8,128,128]{2,1,0:T(8,128)(2,1)S(1)} %get-tuple-element.70), channel_id=1, source_target_pairs={{0,2},{1,3},{2,4},{3,5},{4,6},{5,7},{6,8},{7,9},{8,10},{9,11},{10,... | collective-permute-start | bytes 786440 | tf_op jit(solution)/shard_map/ppermute | solution.py:463
  57.4 9.8 %collective-permute-start.21 = (bf16[8,128,128]{2,1,0:T(8,128)(2,1)S(1)}, bf16[8,128,128]{2,1,0:T(8,128)(2,1)S(1)}, u32[]{:S(2)}, u32[]{:S(2)}) collective-permute-start(bf16[8,128,128]{2,1,0:T(8,128)(2,1)S(1)} %get-tuple-element.71), channel_id=1, source_target_pairs={{0,1},{1,0},{2,3},{3,2},{4,5},{5,4},{6,7},{7,6},{8,9},{9,8},{10,11... | collective-permute-start | bytes 786440 | tf_op jit(solution)/shard_map/ppermute | solution.py:453
  58.8 8.6 %collective-permute-start.22 = (bf16[8,128,128]{2,1,0:T(8,128)(2,1)S(1)}, bf16[8,128,128]{2,1,0:T(8,128)(2,1)S(1)}, u32[]{:S(2)}, u32[]{:S(2)}) collective-permute-start(bf16[8,128,128]{2,1,0:T(8,128)(2,1)S(1)} %get-tuple-element.72), channel_id=1, source_target_pairs={{0,14},{1,15},{2,0},{3,1},{4,2},{5,3},{6,4},{7,5},{8,6},{9,7},{10,... | collective-permute-start | bytes 786440 | tf_op jit(solution)/shard_map/ppermute | solution.py:463
  63.3 13.2 %collective-permute-start.14 = (bf16[16,128,128]{2,1,0:T(8,128)(2,1)S(1)}, bf16[16,128,128]{2,1,0:T(8,128)(2,1)S(1)}, u32[]{:S(2)}, u32[]{:S(2)}) collective-permute-start(bf16[16,128,128]{2,1,0:T(8,128)(2,1)S(1)} %get-tuple-element.67), channel_id=1, source_target_pairs={{0,1},{1,0},{2,3},{3,2},{4,5},{5,4},{6,7},{7,6},{8,9},{9,8},{10,11... | collective-permute-start | bytes 1572872 | tf_op jit(solution)/shard_map/ppermute | solution.py:453
  67.1 13.1 %collective-permute-start.18 = (bf16[16,128,128]{2,1,0:T(8,128)(2,1)S(1)}, bf16[16,128,128]{2,1,0:T(8,128)(2,1)S(1)}, u32[]{:S(2)}, u32[]{:S(2)}) collective-permute-start(bf16[16,128,128]{2,1,0:T(8,128)(2,1)S(1)} %hop_3.1), channel_id=1, source_target_pairs={{0,2},{1,3},{2,4},{3,5},{4,6},{5,7},{6,8},{7,9},{8,10},{9,11},{10,... | collective-permute-start | bytes 1572872 | tf_op jit(solution)/shard_map/ppermute | solution.py:463
  67.6 15.2 %collective-permute-start.23 = (bf16[16,128,128]{2,1,0:T(8,128)(2,1)S(1)}, bf16[16,128,128]{2,1,0:T(8,128)(2,1)S(1)}, u32[]{:S(2)}, u32[]{:S(2)}) collective-permute-start(bf16[16,128,128]{2,1,0:T(8,128)(2,1)S(1)} %hop_5.1), channel_id=1, source_target_pairs={{0,14},{1,15},{2,0},{3,1},{4,2},{5,3},{6,4},{7,5},{8,6},{9,7},{10,... | collective-permute-start | bytes 1572872 | tf_op jit(solution)/shard_map/ppermute | solution.py:463
  72.6 15.5 %collective-permute-start.13 = (bf16[16,128,128]{2,1,0:T(8,128)(2,1)S(1)}, bf16[16,128,128]{2,1,0:T(8,128)(2,1)S(1)}, u32[]{:S(2)}, u32[]{:S(2)}) collective-permute-start(bf16[16,128,128]{2,1,0:T(8,128)(2,1)S(1)} %get-tuple-element.66), channel_id=1, source_target_pairs={{0,1},{1,0},{2,3},{3,2},{4,5},{5,4},{6,7},{7,6},{8,9},{9,8},{10,11... | collective-permute-start | bytes 1572872 | tf_op jit(solution)/shard_map/ppermute | solution.py:453
  80.4 13.7 %collective-permute-start.19 = (bf16[16,128,128]{2,1,0:T(8,128)(2,1)S(1)}, bf16[16,128,128]{2,1,0:T(8,128)(2,1)S(1)}, u32[]{:S(2)}, u32[]{:S(2)}) collective-permute-start(bf16[16,128,128]{2,1,0:T(8,128)(2,1)S(1)} %hop_2.1), channel_id=1, source_target_pairs={{0,2},{1,3},{2,4},{3,5},{4,6},{5,7},{6,8},{7,9},{8,10},{9,11},{10,... | collective-permute-start | bytes 1572872 | tf_op jit(solution)/shard_map/ppermute | solution.py:463
  83.0 12.7 %collective-permute-start.24 = (bf16[16,128,128]{2,1,0:T(8,128)(2,1)S(1)}, bf16[16,128,128]{2,1,0:T(8,128)(2,1)S(1)}, u32[]{:S(2)}, u32[]{:S(2)}) collective-permute-start(bf16[16,128,128]{2,1,0:T(8,128)(2,1)S(1)} %hop_6.1), channel_id=1, source_target_pairs={{0,14},{1,15},{2,0},{3,1},{4,2},{5,3},{6,4},{7,5},{8,6},{9,7},{10,... | collective-permute-start | bytes 1572872 | tf_op jit(solution)/shard_map/ppermute | solution.py:463
  94.2 13.5 %copy-start.2 = (bf16[128,256]{1,0:T(8,128)(2,1)S(1)}, bf16[128,256]{1,0:T(8,128)(2,1)}, u32[]{:S(2)}) copy-start(bf16[128,256]{1,0:T(8,128)(2,1)} %weight.1) | copy-start | bytes 196612
  94.2 13.5 %copy-start.3 = (f32[256]{0:T(256)S(1)}, f32[256]{0:T(256)}, u32[]{:S(2)}) copy-start(f32[256]{0:T(256)} %param.13) | copy-start | bytes 3076
  94.2 12.0 %collective-permute-start.20 = (bf16[16,128,128]{2,1,0:T(8,128)(2,1)S(1)}, bf16[16,128,128]{2,1,0:T(8,128)(2,1)S(1)}, u32[]{:S(2)}, u32[]{:S(2)}) collective-permute-start(bf16[16,128,128]{2,1,0:T(8,128)(2,1)S(1)} %hop_1.1), channel_id=1, source_target_pairs={{0,2},{1,3},{2,4},{3,5},{4,6},{5,7},{6,8},{7,9},{8,10},{9,11},{10,... | collective-permute-start | bytes 1572872 | tf_op jit(solution)/shard_map/ppermute | solution.py:476
  95.9 11.8 %collective-permute-start.25 = (bf16[16,128,128]{2,1,0:T(8,128)(2,1)S(1)}, bf16[16,128,128]{2,1,0:T(8,128)(2,1)S(1)}, u32[]{:S(2)}, u32[]{:S(2)}) collective-permute-start(bf16[16,128,128]{2,1,0:T(8,128)(2,1)S(1)} %hop_7.1), channel_id=1, source_target_pairs={{0,14},{1,15},{2,0},{3,1},{4,2},{5,3},{6,4},{7,5},{8,6},{9,7},{10,... | collective-permute-start | bytes 1572872 | tf_op jit(solution)/shard_map/ppermute | solution.py:476
  99.4 6.7 %collective-permute-start.12 = (bf16[8,128,128]{2,1,0:T(8,128)(2,1)S(1)}, bf16[8,128,128]{2,1,0:T(8,128)(2,1)S(1)}, u32[]{:S(2)}, u32[]{:S(2)}) collective-permute-start(bf16[8,128,128]{2,1,0:T(8,128)(2,1)S(1)} %get-tuple-element.65), channel_id=1, source_target_pairs={{0,1},{1,0},{2,3},{3,2},{4,5},{5,4},{6,7},{7,6},{8,9},{9,8},{10,11... | collective-permute-start | bytes 786440 | tf_op jit(solution)/shard_map/ppermute | solution.py:453

commit v2 on v1

--- a/solution.py
+++ b/solution.py
@@ -124,7 +124,9 @@
     return jnp.where(filled > 0, row, spare), starts.astype(jnp.int32), counts.astype(jnp.int32)
 
 
-def plan_kernel(where, dest, source, plan):
+def plan_kernel(where, dest, source, kept_plan, same_where, plan, sem):
+    for i in range(5):
+        same_where[i] = where[i]
     my_y, my_x, my_k, my_z, my_xhi = (where[i] for i in range(5))
     block, from_block = dest[...], source[...]
     row = from_block // TPD
@@ -151,15 +153,22 @@
     plan[0:1, :] = row
     plan[1:2, 0:TILE] = starts
     plan[2:3, 0:TILE] = counts
+    copy = pltpu.make_async_copy(plan, kept_plan, sem)
+    copy.start()
+    copy.wait()
 
 
 def make_plan(where, dest, source):
     return call(
         plan_kernel,
         "plan",
-        out_shape=jax.ShapeDtypeStruct((8, WIDTH), jnp.int32),
+        out_shape=[
+            pltpu.SMEM((8, WIDTH), jnp.int32),
+            jax.ShapeDtypeStruct(where.shape, where.dtype),
+        ],
         in_specs=[SMEM_SPEC] + [VMEM_SPEC] * 2,
-        out_specs=VMEM_SPEC,
+        out_specs=[SMEM_SPEC] * 2,
+        scratch_shapes=[VMEM((8, WIDTH), jnp.int32), pltpu.SemaphoreType.DMA(())],
     )(where, dest, source)
 
 
@@ -307,7 +316,7 @@
         in_specs=[SMEM_SPEC] + [VMEM_SPEC] * 2,
         out_specs=[VMEM_SPEC] * 3,
         input_output_aliases={2: 0},
-    )(plan, keep(tiles), keep(feats))
+    )(keep_scalars(plan), keep(tiles), keep(feats))
 
 
 def more_kernel(kinds, n_feats, plan, tiles, *refs):
@@ -326,7 +335,7 @@
         in_specs=[SMEM_SPEC] + [VMEM_SPEC] * (n - 1 + len(accs)),
         out_specs=[VMEM_SPEC] * len(accs),
         input_output_aliases={n + i: i for i in range(len(accs))},
-    )(plan, keep(tiles), *[keep(f) for f in feats], *[keep(acc) for acc in accs])
+    )(keep_scalars(plan), keep(tiles), *[keep(f) for f in feats], *[keep(acc) for acc in accs])
 
 
 def convert_sends(acc, parts, sends):
@@ -354,7 +363,7 @@
         in_specs=[SMEM_SPEC] + [VMEM_SPEC] * 3,
         out_specs=[VMEM_SPEC] * 2,
         input_output_aliases={3: 0},
-    )(plan, keep(tiles), keep(far_sibling), keep(acc))
+    )(keep_scalars(plan), keep(tiles), keep(far_sibling), keep(acc))
     rest = call(
         sends_kernel,
         "other_sends",
@@ -426,8 +435,8 @@
     slot = jnp.arange(SLOTS, dtype=jnp.int32)[None, :]
     dest = jnp.where(slot < tile_count[0, 0], tile_dest[0], -1)
     up, down, side = (send(node_feats, p) for p in (FROM_UP, FROM_DOWN, FROM_SIDE))
-    plan = make_plan(where, dest, tile_source[0])
-    up, down, side, plan = lax.optimization_barrier((up, down, side, plan))
+    plan, where = make_plan(where, dest, tile_source[0])
+    up, down, side, where = lax.optimization_barrier((up, down, side, where))
     far, down_side, up_side = send(up, FROM_UP), send(side, FROM_DOWN), send(up, FROM_SIDE)
     tiles = load_tiles(tile_vals[0, 0])
     feats = pack(None, 0, [node_feats, up, down, side])

time: 111 us -> 108 us (0.973)
  Pallas kernels: 15.9 us -> 12.6 us
  waiting for transfers between devices: 37.9 us -> 39.5 us
    pallas_call x3, Pallas kernels: 6.11 us -> 2.74 us  [more_products(): call(functools.partial(more_kernel, kinds, len(feats)), name, out_shape=[...]
    pallas_call x1, Pallas kernels: 0.98 us -> 2.38 us  [make_plan(): call(plan_kernel, 'plan', out_shape=[pltpu.SMEM((8, WIDTH), jnp.int32), j...]
    ppermute x6, waiting for transfers between devices: 11.2 us -> 12.6 us  [on_device(): part = lax.ppermute(part, 'col', X_FLIP)]
    ppermute x1, waiting for transfers between devices: 0.6 us -> 1.72 us  [on_device(): partner_dest = lax.ppermute(dest, 'col', X_FLIP)]
  transfers between devices with their start and end apart: 26 -> 26, of which waited for: 19 -> 18; matrix products, arithmetic and copies ran while one was open for 1% -> 1% of each run, Pallas kernels for 12% -> 10%
where the time goes in v2:
time: 108 us; the launch traced here: 107 us
  starting transfers between devices  48.6 us (45%)
  waiting for transfers between devices  39.5 us (37%)
  Pallas kernels  12.6 us (12%)
  local copies, waits for them, and re-layouts  4.62 us (4%)
    ppermute x8, starting transfers between devices, on_device(): chains = [lax.ppermute(c, 'col', p) for c, p in zip(chains, Z_CHAINS)]  18.6 us
    ppermute x11, starting transfers between devices, send(): return lax.ppermute(array, 'row', perm)  18.2 us
    ppermute x8, waiting for transfers between devices, on_device(): chains = [lax.ppermute(c, 'col', p) for c, p in zip(chains, Z_CHAINS)]  17 us
    ppermute x6, waiting for transfers between devices, on_device(): part = lax.ppermute(part, 'col', X_FLIP)  12.6 us
    ppermute x6, starting transfers between devices, on_device(): part = lax.ppermute(part, 'col', X_FLIP)  8.5 us
    ppermute x11, waiting for transfers between devices, send(): return lax.ppermute(array, 'row', perm)  8.19 us
    unnamed x10, local copies, waits for them, and re-layouts  4.54 us
    ppermute x1, starting transfers between devices, on_device(): partner_dest = lax.ppermute(dest, 'col', X_FLIP)  3.26 us
  transfers between devices with their start and end apart: 26, of which 18 were waited for; matrix products, arithmetic and copies ran while one was open for 1% of the time, Pallas kernels for 10%

profile of v2, /device:TPU:1, one launch (start us, length us, event | category | flops | bytes accessed | tf_op | source)
XLA Modules:
  0.0 106.9 jit_solution(13214751889985963527)
XLA Ops:
  0.0 2.1 %collective-permute-start.1 = (bf16[2048,128]{1,0:T(8,128)(2,1)}, bf16[2048,128]{1,0:T(8,128)(2,1)S(1)}, u32[]{:S(2)}, u32[]{:S(2)}) collective-permute-start(bf16[2048,128]{1,0:T(8,128)(2,1)} %refs_0_.1), channel_id=1, source_target_pairs={{0,64},{16,80},{32,96},{48,112},{64,128},{80,144},{96,160},{112,17... | collective-permute-start | bytes 1572872 | tf_op jit(solution)/shard_map/ppermute | solution.py:427
  2.1 1.4 %collective-permute-start = (bf16[2048,128]{1,0:T(8,128)(2,1)}, bf16[2048,128]{1,0:T(8,128)(2,1)S(1)}, u32[]{:S(2)}, u32[]{:S(2)}) collective-permute-start(bf16[2048,128]{1,0:T(8,128)(2,1)} %refs_0_.1), channel_id=1, source_target_pairs={{0,192},{16,208},{32,224},{48,240},{64,0},{80,16},{96,32},{112,48}... | collective-permute-start | bytes 1572872 | tf_op jit(solution)/shard_map/ppermute | solution.py:427
  3.6 1.2 %collective-permute-start.2 = (bf16[2048,128]{1,0:T(8,128)(2,1)}, bf16[2048,128]{1,0:T(8,128)(2,1)S(1)}, u32[]{:S(2)}, u32[]{:S(2)}) collective-permute-start(bf16[2048,128]{1,0:T(8,128)(2,1)} %refs_0_.1), channel_id=1, source_target_pairs={{0,32},{16,48},{32,0},{48,16},{64,96},{80,112},{96,64},{112,80},{1... | collective-permute-start | bytes 1572872 | tf_op jit(solution)/shard_map/ppermute | solution.py:427
  5.4 0.1 stack.23.where
  5.5 0.7 compare_select_fusion.dest
  6.2 0.7 copy-done.4
  6.9 2.4 %plan.1 = (s32[8,512]{1,0:T(8,128)S(4)}, s32[5]{0:T(128)S(1)}) custom-call(s32[5]{0:T(128)S(1)} %stack.23.where, s32[1,256]{1,0:T(1,128)S(1)} %compare_select_fusion.dest, s32[1,256]{1,0:T(1,128)S(1)} %bitcast.14), custom_call_target="tpu_custom_call" | custom-call | tf_op jit(solution)/shard_map/plan/pallas_call | solution.py:162
  9.3 4.1 %collective-permute-done.1.refs_2_ = bf16[2048,128]{1,0:T(8,128)(2,1)S(1)} collective-permute-done((bf16[2048,128]{1,0:T(8,128)(2,1)}, bf16[2048,128]{1,0:T(8,128)(2,1)S(1)}, u32[]{:S(2)}, u32[]{:S(2)}) %collective-permute-start.1) | collective-permute-done | bytes 524320 | tf_op jit(solution)/shard_map/ppermute | solution.py:427
  13.4 1.3 %collective-permute-done.refs_1_ = bf16[2048,128]{1,0:T(8,128)(2,1)S(1)} collective-permute-done((bf16[2048,128]{1,0:T(8,128)(2,1)}, bf16[2048,128]{1,0:T(8,128)(2,1)S(1)}, u32[]{:S(2)}, u32[]{:S(2)}) %collective-permute-start) | collective-permute-done | bytes 524320 | tf_op jit(solution)/shard_map/ppermute | solution.py:427
  14.6 0.2 collective-permute-done.2.refs_3_
  14.9 1.3 %collective-permute-start.4 = (bf16[2048,128]{1,0:T(8,128)(2,1)S(1)}, bf16[2048,128]{1,0:T(8,128)(2,1)S(1)}, u32[]{:S(2)}, u32[]{:S(2)}) collective-permute-start(bf16[2048,128]{1,0:T(8,128)(2,1)S(1)} %collective-permute-done.2.refs_3_), channel_id=1, source_target_pairs={{0,64},{16,80},{32,96},{48,112},{64,128},{80,144},{96,160},{112,17... | collective-permute-start | bytes 1572872 | tf_op jit(solution)/shard_map/ppermute | solution.py:427
  16.1 1.2 %collective-permute-start.5 = (bf16[2048,128]{1,0:T(8,128)(2,1)S(1)}, bf16[2048,128]{1,0:T(8,128)(2,1)S(1)}, u32[]{:S(2)}, u32[]{:S(2)}) collective-permute-start(bf16[2048,128]{1,0:T(8,128)(2,1)S(1)} %collective-permute-done.refs_1_), channel_id=1, source_target_pairs={{0,32},{16,48},{32,0},{48,16},{64,96},{80,112},{96,64},{112,80},{1... | collective-permute-start | bytes 1572872 | tf_op jit(solution)/shard_map/ppermute | solution.py:427
  17.3 2.3 %collective-permute-start.3 = (bf16[2048,128]{1,0:T(8,128)(2,1)S(1)}, bf16[2048,128]{1,0:T(8,128)(2,1)S(1)}, u32[]{:S(2)}, u32[]{:S(2)}) collective-permute-start(bf16[2048,128]{1,0:T(8,128)(2,1)S(1)} %collective-permute-done.refs_1_), channel_id=1, source_target_pairs={{0,192},{16,208},{32,224},{48,240},{64,0},{80,16},{96,32},{112,48}... | collective-permute-start | bytes 1572872 | tf_op jit(solution)/shard_map/ppermute | solution.py:427
  19.6 3.4 %copy-done = bf16[1,1,256,128,128]{4,3,2,1,0:T(8,128)(2,1)S(1)} copy-done((bf16[1,1,256,128,128]{4,3,2,1,0:T(8,128)(2,1)S(1)}, bf16[1,1,256,128,128]{4,3,2,1,0:T(8,128)(2,1)}, u32[]{:S(2)}) %copy-start) | copy-done | bytes 8388632
  23.0 0.6 load_tiles.1.tiles
  23.6 0.5 copy-done.1
  24.1 0.1 pack.1.feats
  24.2 2.1 %first_products.1 = (bf16[14336,128]{1,0:T(8,128)(2,1)S(1)}, f32[65,128,128]{2,1,0:T(8,128)S(1)}, f32[129,128,128]{2,1,0:T(8,128)S(1)}) custom-call(s32[8,512]{1,0:T(8,128)S(4)} %get-tuple-element.45.plan, bf16[256,128,128]{2,1,0:T(8,128)(2,1)S(1)} %load_tiles.1.tiles, bf16[14336,128]{1,0:T(8,128)(2,1)S(1)} %pack.1.feats), custom_call_target="tpu_custom_call", output_to_operand_aliasing={{0}: (2, {})} | custom-call | tf_op jit(solution)/shard_map/first_products/pallas_call | solution.py:308
  26.3 0.9 collective-permute-done.5.up_side
  27.2 0.9 collective-permute-done.3.far
  28.1 0.1 pack_second.1
  28.3 3.7 %collective-permute-start.10 = (bf16[14336,128]{1,0:T(8,128)(2,1)S(1)}, bf16[14336,128]{1,0:T(8,128)(2,1)S(1)}, u32[]{:S(2)}, u32[]{:S(2)}) collective-permute-start(bf16[14336,128]{1,0:T(8,128)(2,1)S(1)} %get-tuple-element.57.refs_0_), channel_id=1, source_target_pairs={{0,16},{16,0},{32,48},{48,32},{64,80},{80,64},{96,112},{112,96},{1... | collective-permute-start | bytes 11010056 | tf_op jit(solution)/shard_map/ppermute | solution.py:427
  32.0 1.1 %collective-permute-start.7 = (bf16[880,128]{1,0:T(8,128)(2,1)S(1)}, bf16[880,128]{1,0:T(8,128)(2,1)S(1)}, u32[]{:S(2)}, u32[]{:S(2)}) collective-permute-start(bf16[880,128]{1,0:T(8,128)(2,1)S(1)} %get-tuple-element.55), channel_id=1, source_target_pairs={{0,64},{16,80},{32,96},{48,112},{64,128},{80,144},{96,160},{112,17... | collective-permute-start | bytes 675848 | tf_op jit(solution)/shard_map/ppermute | solution.py:427
  33.1 2.3 %collective-permute-start.6 = (bf16[752,128]{1,0:T(8,128)(2,1)S(1)}, bf16[752,128]{1,0:T(8,128)(2,1)S(1)}, u32[]{:S(2)}, u32[]{:S(2)}) collective-permute-start(bf16[752,128]{1,0:T(8,128)(2,1)S(1)} %get-tuple-element.54), channel_id=1, source_target_pairs={{0,192},{16,208},{32,224},{48,240},{64,0},{80,16},{96,32},{112,48}... | collective-permute-start | bytes 577544 | tf_op jit(solution)/shard_map/ppermute | solution.py:427
  35.4 3.3 %collective-permute-start.9 = (s32[1,256]{1,0:T(1,128)S(1)}, s32[1,256]{1,0:T(1,128)S(1)}, u32[]{:S(2)}, u32[]{:S(2)}) collective-permute-start(s32[1,256]{1,0:T(1,128)S(1)} %compare_select_fusion.dest), channel_id=1, source_target_pairs={{0,1},{1,0},{2,3},{3,2},{4,5},{5,4},{6,7},{7,6},{8,9},{9,8},{10,11... | collective-permute-start | bytes 3080 | tf_op jit(solution)/shard_map/ppermute | solution.py:447
  38.7 0.6 late_products.1
  39.3 1.7 %collective-permute-done.9.partner_dest = s32[1,256]{1,0:T(1,128)S(1)} collective-permute-done((s32[1,256]{1,0:T(1,128)S(1)}, s32[1,256]{1,0:T(1,128)S(1)}, u32[]{:S(2)}, u32[]{:S(2)}) %collective-permute-start.9) | collective-permute-done | bytes 1056 | tf_op jit(solution)/shard_map/ppermute | solution.py:447
  41.0 0.2 collective-permute-done.7.refs_1_
  41.2 1.5 %collective-permute-start.11 = (bf16[2048,128]{1,0:T(8,128)(2,1)S(1)}, bf16[2048,128]{1,0:T(8,128)(2,1)S(1)}, u32[]{:S(2)}, u32[]{:S(2)}) collective-permute-start(bf16[2048,128]{1,0:T(8,128)(2,1)S(1)} %join.1.refs_1_), channel_id=1, source_target_pairs={{0,16},{16,0},{32,48},{48,32},{64,80},{80,64},{96,112},{112,96},{1... | collective-permute-start | bytes 1572872 | tf_op jit(solution)/shard_map/ppermute | solution.py:427
  42.8 0.9 other_half.1._
  43.7 0.6 collective-permute-done.11.refs_2_.far_sibling
  44.3 0.3 first_send.1
  44.6 2.1 %collective-permute-start.16 = (bf16[8,128,128]{2,1,0:T(8,128)(2,1)S(1)}, bf16[8,128,128]{2,1,0:T(8,128)(2,1)S(1)}, u32[]{:S(2)}, u32[]{:S(2)}) collective-permute-start(bf16[8,128,128]{2,1,0:T(8,128)(2,1)S(1)} %get-tuple-element.73), channel_id=1, source_target_pairs={{0,1},{1,0},{2,3},{3,2},{4,5},{5,4},{6,7},{7,6},{8,9},{9,8},{10,11... | collective-permute-start | bytes 786440 | tf_op jit(solution)/shard_map/ppermute | solution.py:462
  46.7 1.3 %partner_map.1.slots = s32[1,128]{1,0:T(1,128)S(4)} custom-call(s32[5]{0:T(128)S(1)} %get-tuple-element.42.where, s32[1,256]{1,0:T(1,128)S(1)} %collective-permute-done.9.partner_dest), custom_call_target="tpu_custom_call" | custom-call | tf_op jit(solution)/shard_map/partner_map/pallas_call | solution.py:188
  48.0 0.2 other_sends.1
  48.2 1.3 %collective-permute-start.15 = (bf16[8,128,128]{2,1,0:T(8,128)(2,1)S(1)}, bf16[8,128,128]{2,1,0:T(8,128)(2,1)S(1)}, u32[]{:S(2)}, u32[]{:S(2)}) collective-permute-start(bf16[8,128,128]{2,1,0:T(8,128)(2,1)S(1)} %get-tuple-element.72), channel_id=1, source_target_pairs={{0,1},{1,0},{2,3},{3,2},{4,5},{5,4},{6,7},{7,6},{8,9},{9,8},{10,11... | collective-permute-start | bytes 786440 | tf_op jit(solution)/shard_map/ppermute | solution.py:462
  49.5 1.2 %own_half.1.own = f32[129,128,128]{2,1,0:T(8,128)S(1)} custom-call(s32[8,512]{1,0:T(8,128)S(4)} %get-tuple-element.45.plan, bf16[256,128,128]{2,1,0:T(8,128)(2,1)S(1)} %load_tiles.1.tiles, bf16[14336,128]{1,0:T(8,128)(2,1)S(1)} %collective-permute-done.10.refs_0_, bf16[2048,128]{1,0:T(8,128)(2,1)S(1)} %join.1.refs_1_, ...), custom_call_target="tpu_custom_call", output_to_operand_aliasing={{}: (5, {})} | custom-call | tf_op jit(solution)/shard_map/own_half/pallas_call | solution.py:331
  50.7 3.0 %collective-permute-done.16.arrived = bf16[8,128,128]{2,1,0:T(8,128)(2,1)S(1)} collective-permute-done((bf16[8,128,128]{2,1,0:T(8,128)(2,1)S(1)}, bf16[8,128,128]{2,1,0:T(8,128)(2,1)S(1)}, u32[]{:S(2)}, u32[]{:S(2)}) %collective-permute-start.16) | collective-permute-done | bytes 262176 | tf_op jit(solution)/shard_map/ppermute | solution.py:462
  53.7 0.1 hop_4.1
  53.9 1.8 %collective-permute-start.17 = (bf16[8,128,128]{2,1,0:T(8,128)(2,1)S(1)}, bf16[8,128,128]{2,1,0:T(8,128)(2,1)S(1)}, u32[]{:S(2)}, u32[]{:S(2)}) collective-permute-start(bf16[8,128,128]{2,1,0:T(8,128)(2,1)S(1)} %get-tuple-element.74), channel_id=1, source_target_pairs={{0,2},{1,3},{2,4},{3,5},{4,6},{5,7},{6,8},{7,9},{8,10},{9,11},{10,... | collective-permute-start | bytes 786440 | tf_op jit(solution)/shard_map/ppermute | solution.py:472
  55.6 1.9 %collective-permute-start.21 = (bf16[8,128,128]{2,1,0:T(8,128)(2,1)S(1)}, bf16[8,128,128]{2,1,0:T(8,128)(2,1)S(1)}, u32[]{:S(2)}, u32[]{:S(2)}) collective-permute-start(bf16[8,128,128]{2,1,0:T(8,128)(2,1)S(1)} %get-tuple-element.75), channel_id=1, source_target_pairs={{0,1},{1,0},{2,3},{3,2},{4,5},{5,4},{6,7},{7,6},{8,9},{9,8},{10,11... | collective-permute-start | bytes 786440 | tf_op jit(solution)/shard_map/ppermute | solution.py:462
  57.6 4.0 %collective-permute-start.22 = (bf16[8,128,128]{2,1,0:T(8,128)(2,1)S(1)}, bf16[8,128,128]{2,1,0:T(8,128)(2,1)S(1)}, u32[]{:S(2)}, u32[]{:S(2)}) collective-permute-start(bf16[8,128,128]{2,1,0:T(8,128)(2,1)S(1)} %get-tuple-element.76), channel_id=1, source_target_pairs={{0,14},{1,15},{2,0},{3,1},{4,2},{5,3},{6,4},{7,5},{8,6},{9,7},{10,... | collective-permute-start | bytes 786440 | tf_op jit(solution)/shard_map/ppermute | solution.py:472
  61.6 1.3 %collective-permute-start.14 = (bf16[16,128,128]{2,1,0:T(8,128)(2,1)S(1)}, bf16[16,128,128]{2,1,0:T(8,128)(2,1)S(1)}, u32[]{:S(2)}, u32[]{:S(2)}) collective-permute-start(bf16[16,128,128]{2,1,0:T(8,128)(2,1)S(1)} %get-tuple-element.71), channel_id=1, source_target_pairs={{0,1},{1,0},{2,3},{3,2},{4,5},{5,4},{6,7},{7,6},{8,9},{9,8},{10,11... | collective-permute-start | bytes 1572872 | tf_op jit(solution)/shard_map/ppermute | solution.py:462
  62.9 2.2 %collective-permute-done.17.refs_0_ = bf16[8,128,128]{2,1,0:T(8,128)(2,1)S(1)} collective-permute-done((bf16[8,128,128]{2,1,0:T(8,128)(2,1)S(1)}, bf16[8,128,128]{2,1,0:T(8,128)(2,1)S(1)}, u32[]{:S(2)}, u32[]{:S(2)}) %collective-permute-start.17) | collective-permute-done | bytes 262176 | tf_op jit(solution)/shard_map/ppermute | solution.py:472
  65.2 0.2 hop_3.1
  65.4 0.2 hop_5.1
  65.6 5.5 %collective-permute-start.23 = (bf16[16,128,128]{2,1,0:T(8,128)(2,1)S(1)}, bf16[16,128,128]{2,1,0:T(8,128)(2,1)S(1)}, u32[]{:S(2)}, u32[]{:S(2)}) collective-permute-start(bf16[16,128,128]{2,1,0:T(8,128)(2,1)S(1)} %hop_5.1), channel_id=1, source_target_pairs={{0,14},{1,15},{2,0},{3,1},{4,2},{5,3},{6,4},{7,5},{8,6},{9,7},{10,... | collective-permute-start | bytes 1572872 | tf_op jit(solution)/shard_map/ppermute | solution.py:472
  71.1 1.6 %collective-permute-start.13 = (bf16[16,128,128]{2,1,0:T(8,128)(2,1)S(1)}, bf16[16,128,128]{2,1,0:T(8,128)(2,1)S(1)}, u32[]{:S(2)}, u32[]{:S(2)}) collective-permute-start(bf16[16,128,128]{2,1,0:T(8,128)(2,1)S(1)} %get-tuple-element.70), channel_id=1, source_target_pairs={{0,1},{1,0},{2,3},{3,2},{4,5},{5,4},{6,7},{7,6},{8,9},{9,8},{10,11... | collective-permute-start | bytes 1572872 | tf_op jit(solution)/shard_map/ppermute | solution.py:462
  72.8 1.2 %collective-permute-done.14.arrived = bf16[16,128,128]{2,1,0:T(8,128)(2,1)S(1)} collective-permute-done((bf16[16,128,128]{2,1,0:T(8,128)(2,1)S(1)}, bf16[16,128,128]{2,1,0:T(8,128)(2,1)S(1)}, u32[]{:S(2)}, u32[]{:S(2)}) %collective-permute-start.14) | collective-permute-done | bytes 524320 | tf_op jit(solution)/shard_map/ppermute | solution.py:462
  74.0 4.1 %collective-permute-done.18.refs_0_ = bf16[16,128,128]{2,1,0:T(8,128)(2,1)S(1)} collective-permute-done((bf16[16,128,128]{2,1,0:T(8,128)(2,1)S(1)}, bf16[16,128,128]{2,1,0:T(8,128)(2,1)S(1)}, u32[]{:S(2)}, u32[]{:S(2)}) %collective-permute-start.18) | collective-permute-done | bytes 524320 | tf_op jit(solution)/shard_map/ppermute | solution.py:472
  78.0 0.2 hop_2.1
  78.3 2.7 %collective-permute-done.23.refs_0_ = bf16[16,128,128]{2,1,0:T(8,128)(2,1)S(1)} collective-permute-done((bf16[16,128,128]{2,1,0:T(8,128)(2,1)S(1)}, bf16[16,128,128]{2,1,0:T(8,128)(2,1)S(1)}, u32[]{:S(2)}, u32[]{:S(2)}) %collective-permute-start.23) | collective-permute-done | bytes 524320 | tf_op jit(solution)/shard_map/ppermute | solution.py:472
  81.0 0.2 hop_6.1
  81.2 3.5 %collective-permute-start.24 = (bf16[16,128,128]{2,1,0:T(8,128)(2,1)S(1)}, bf16[16,128,128]{2,1,0:T(8,128)(2,1)S(1)}, u32[]{:S(2)}, u32[]{:S(2)}) collective-permute-start(bf16[16,128,128]{2,1,0:T(8,128)(2,1)S(1)} %hop_6.1), channel_id=1, source_target_pairs={{0,14},{1,15},{2,0},{3,1},{4,2},{5,3},{6,4},{7,5},{8,6},{9,7},{10,... | collective-permute-start | bytes 1572872 | tf_op jit(solution)/shard_map/ppermute | solution.py:472
  84.7 1.9 %collective-permute-done.13.arrived = bf16[16,128,128]{2,1,0:T(8,128)(2,1)S(1)} collective-permute-done((bf16[16,128,128]{2,1,0:T(8,128)(2,1)S(1)}, bf16[16,128,128]{2,1,0:T(8,128)(2,1)S(1)}, u32[]{:S(2)}, u32[]{:S(2)}) %collective-permute-start.13) | collective-permute-done | bytes 524320 | tf_op jit(solution)/shard_map/ppermute | solution.py:462
  86.6 6.2 %collective-permute-done.19.refs_0_ = bf16[16,128,128]{2,1,0:T(8,128)(2,1)S(1)} collective-permute-done((bf16[16,128,128]{2,1,0:T(8,128)(2,1)S(1)}, bf16[16,128,128]{2,1,0:T(8,128)(2,1)S(1)}, u32[]{:S(2)}, u32[]{:S(2)}) %collective-permute-start.19) | collective-permute-done | bytes 524320 | tf_op jit(solution)/shard_map/ppermute | solution.py:472
  92.9 0.2 hop_1.1
  93.2 0.5 collective-permute-done.24.refs_0_
  93.7 0.2 hop_7.1
  93.9 3.5 %collective-permute-start.25 = (bf16[16,128,128]{2,1,0:T(8,128)(2,1)S(1)}, bf16[16,128,128]{2,1,0:T(8,128)(2,1)S(1)}, u32[]{:S(2)}, u32[]{:S(2)}) collective-permute-start(bf16[16,128,128]{2,1,0:T(8,128)(2,1)S(1)} %hop_7.1), channel_id=1, source_target_pairs={{0,14},{1,15},{2,0},{3,1},{4,2},{5,3},{6,4},{7,5},{8,6},{9,7},{10,... | collective-permute-start | bytes 1572872 | tf_op jit(solution)/shard_map/ppermute | solution.py:485
  97.3 0.3 collective-permute-start.12
  97.6 6.4 %collective-permute-done.12.arrived = bf16[8,128,128]{2,1,0:T(8,128)(2,1)S(1)} collective-permute-done((bf16[8,128,128]{2,1,0:T(8,128)(2,1)S(1)}, bf16[8,128,128]{2,1,0:T(8,128)(2,1)S(1)}, u32[]{:S(2)}, u32[]{:S(2)}) %collective-permute-start.12) | collective-permute-done | bytes 262176 | tf_op jit(solution)/shard_map/ppermute | solution.py:462
  104.1 1.3 %collective-permute-done.20.passed_a = bf16[16,128,128]{2,1,0:T(8,128)(2,1)S(1)} collective-permute-done((bf16[16,128,128]{2,1,0:T(8,128)(2,1)S(1)}, bf16[16,128,128]{2,1,0:T(8,128)(2,1)S(1)}, u32[]{:S(2)}, u32[]{:S(2)}) %collective-permute-start.20) | collective-permute-done | bytes 524320 | tf_op jit(solution)/shard_map/ppermute | solution.py:485
  105.4 1.5 %last.1 = bf16[2048,256]{1,0:T(8,128)(2,1)} custom-call(s32[1,128]{1,0:T(1,128)S(4)} %partner_map.1.slots, f32[129,128,128]{2,1,0:T(8,128)S(1)} %own_half.1.own, bf16[8,128,128]{2,1,0:T(8,128)(2,1)S(1)} %collective-permute-done.12.arrived, bf16[16,128,128]{2,1,0:T(8,128)(2,1)S(1)} %collective-permute-done.20.passed_a, ...), custom_call_target="tpu_custom_call" | custom-call | tf_op jit(solution)/shard_map/last/pallas_call | solution.py:417
  (20 shorter events, 0.3 us)
Async XLA Ops:
  0.0 13.4 %collective-permute-start.1 = (bf16[2048,128]{1,0:T(8,128)(2,1)}, bf16[2048,128]{1,0:T(8,128)(2,1)S(1)}, u32[]{:S(2)}, u32[]{:S(2)}) collective-permute-start(bf16[2048,128]{1,0:T(8,128)(2,1)} %refs_0_.1), channel_id=1, source_target_pairs={{0,64},{16,80},{32,96},{48,112},{64,128},{80,144},{96,160},{112,17... | collective-permute-start | bytes 1572872 | tf_op jit(solution)/shard_map/ppermute | solution.py:427
  2.1 12.5 %collective-permute-start = (bf16[2048,128]{1,0:T(8,128)(2,1)}, bf16[2048,128]{1,0:T(8,128)(2,1)S(1)}, u32[]{:S(2)}, u32[]{:S(2)}) collective-permute-start(bf16[2048,128]{1,0:T(8,128)(2,1)} %refs_0_.1), channel_id=1, source_target_pairs={{0,192},{16,208},{32,224},{48,240},{64,0},{80,16},{96,32},{112,48}... | collective-permute-start | bytes 1572872 | tf_op jit(solution)/shard_map/ppermute | solution.py:427
  3.6 11.3 %collective-permute-start.2 = (bf16[2048,128]{1,0:T(8,128)(2,1)}, bf16[2048,128]{1,0:T(8,128)(2,1)S(1)}, u32[]{:S(2)}, u32[]{:S(2)}) collective-permute-start(bf16[2048,128]{1,0:T(8,128)(2,1)} %refs_0_.1), channel_id=1, source_target_pairs={{0,32},{16,48},{32,0},{48,16},{64,96},{80,112},{96,64},{112,80},{1... | collective-permute-start | bytes 1572872 | tf_op jit(solution)/shard_map/ppermute | solution.py:427
  6.2 0.7 copy-start.4
  14.9 11.5 %collective-permute-start.4 = (bf16[2048,128]{1,0:T(8,128)(2,1)S(1)}, bf16[2048,128]{1,0:T(8,128)(2,1)S(1)}, u32[]{:S(2)}, u32[]{:S(2)}) collective-permute-start(bf16[2048,128]{1,0:T(8,128)(2,1)S(1)} %collective-permute-done.2.refs_3_), channel_id=1, source_target_pairs={{0,64},{16,80},{32,96},{48,112},{64,128},{80,144},{96,160},{112,17... | collective-permute-start | bytes 1572872 | tf_op jit(solution)/shard_map/ppermute | solution.py:427
  16.1 11.1 %collective-permute-start.5 = (bf16[2048,128]{1,0:T(8,128)(2,1)S(1)}, bf16[2048,128]{1,0:T(8,128)(2,1)S(1)}, u32[]{:S(2)}, u32[]{:S(2)}) collective-permute-start(bf16[2048,128]{1,0:T(8,128)(2,1)S(1)} %collective-permute-done.refs_1_), channel_id=1, source_target_pairs={{0,32},{16,48},{32,0},{48,16},{64,96},{80,112},{96,64},{112,80},{1... | collective-permute-start | bytes 1572872 | tf_op jit(solution)/shard_map/ppermute | solution.py:427
  17.3 10.8 %collective-permute-start.3 = (bf16[2048,128]{1,0:T(8,128)(2,1)S(1)}, bf16[2048,128]{1,0:T(8,128)(2,1)S(1)}, u32[]{:S(2)}, u32[]{:S(2)}) collective-permute-start(bf16[2048,128]{1,0:T(8,128)(2,1)S(1)} %collective-permute-done.refs_1_), channel_id=1, source_target_pairs={{0,192},{16,208},{32,224},{48,240},{64,0},{80,16},{96,32},{112,48}... | collective-permute-start | bytes 1572872 | tf_op jit(solution)/shard_map/ppermute | solution.py:427
  19.6 3.4 %copy-start = (bf16[1,1,256,128,128]{4,3,2,1,0:T(8,128)(2,1)S(1)}, bf16[1,1,256,128,128]{4,3,2,1,0:T(8,128)(2,1)}, u32[]{:S(2)}) copy-start(bf16[1,1,256,128,128]{4,3,2,1,0:T(8,128)(2,1)} %param.8) | copy-start | bytes 25165828
  23.0 1.0 copy-start.1
  28.3 14.5 %collective-permute-start.10 = (bf16[14336,128]{1,0:T(8,128)(2,1)S(1)}, bf16[14336,128]{1,0:T(8,128)(2,1)S(1)}, u32[]{:S(2)}, u32[]{:S(2)}) collective-permute-start(bf16[14336,128]{1,0:T(8,128)(2,1)S(1)} %get-tuple-element.57.refs_0_), channel_id=1, source_target_pairs={{0,16},{16,0},{32,48},{48,32},{64,80},{80,64},{96,112},{112,96},{1... | collective-permute-start | bytes 11010056 | tf_op jit(solution)/shard_map/ppermute | solution.py:427
  32.0 9.2 %collective-permute-start.7 = (bf16[880,128]{1,0:T(8,128)(2,1)S(1)}, bf16[880,128]{1,0:T(8,128)(2,1)S(1)}, u32[]{:S(2)}, u32[]{:S(2)}) collective-permute-start(bf16[880,128]{1,0:T(8,128)(2,1)S(1)} %get-tuple-element.55), channel_id=1, source_target_pairs={{0,64},{16,80},{32,96},{48,112},{64,128},{80,144},{96,160},{112,17... | collective-permute-start | bytes 675848 | tf_op jit(solution)/shard_map/ppermute | solution.py:427
  33.1 8.0 %collective-permute-start.6 = (bf16[752,128]{1,0:T(8,128)(2,1)S(1)}, bf16[752,128]{1,0:T(8,128)(2,1)S(1)}, u32[]{:S(2)}, u32[]{:S(2)}) collective-permute-start(bf16[752,128]{1,0:T(8,128)(2,1)S(1)} %get-tuple-element.54), channel_id=1, source_target_pairs={{0,192},{16,208},{32,224},{48,240},{64,0},{80,16},{96,32},{112,48}... | collective-permute-start | bytes 577544 | tf_op jit(solution)/shard_map/ppermute | solution.py:427
  35.4 5.6 %collective-permute-start.8 = (bf16[416,128]{1,0:T(8,128)(2,1)S(1)}, bf16[416,128]{1,0:T(8,128)(2,1)S(1)}, u32[]{:S(2)}, u32[]{:S(2)}) collective-permute-start(bf16[416,128]{1,0:T(8,128)(2,1)S(1)} %get-tuple-element.56), channel_id=1, source_target_pairs={{0,32},{16,48},{32,0},{48,16},{64,96},{80,112},{96,64},{112,80},{1... | collective-permute-start | bytes 319496 | tf_op jit(solution)/shard_map/ppermute | solution.py:427
  35.4 5.6 %collective-permute-start.9 = (s32[1,256]{1,0:T(1,128)S(1)}, s32[1,256]{1,0:T(1,128)S(1)}, u32[]{:S(2)}, u32[]{:S(2)}) collective-permute-start(s32[1,256]{1,0:T(1,128)S(1)} %compare_select_fusion.dest), channel_id=1, source_target_pairs={{0,1},{1,0},{2,3},{3,2},{4,5},{5,4},{6,7},{7,6},{8,9},{9,8},{10,11... | collective-permute-start | bytes 3080 | tf_op jit(solution)/shard_map/ppermute | solution.py:447
  41.2 3.1 %collective-permute-start.11 = (bf16[2048,128]{1,0:T(8,128)(2,1)S(1)}, bf16[2048,128]{1,0:T(8,128)(2,1)S(1)}, u32[]{:S(2)}, u32[]{:S(2)}) collective-permute-start(bf16[2048,128]{1,0:T(8,128)(2,1)S(1)} %join.1.refs_1_), channel_id=1, source_target_pairs={{0,16},{16,0},{32,48},{48,32},{64,80},{80,64},{96,112},{112,96},{1... | collective-permute-start | bytes 1572872 | tf_op jit(solution)/shard_map/ppermute | solution.py:427
  44.6 9.1 %collective-permute-start.16 = (bf16[8,128,128]{2,1,0:T(8,128)(2,1)S(1)}, bf16[8,128,128]{2,1,0:T(8,128)(2,1)S(1)}, u32[]{:S(2)}, u32[]{:S(2)}) collective-permute-start(bf16[8,128,128]{2,1,0:T(8,128)(2,1)S(1)} %get-tuple-element.73), channel_id=1, source_target_pairs={{0,1},{1,0},{2,3},{3,2},{4,5},{5,4},{6,7},{7,6},{8,9},{9,8},{10,11... | collective-permute-start | bytes 786440 | tf_op jit(solution)/shard_map/ppermute | solution.py:462
  48.2 14.7 %collective-permute-start.15 = (bf16[8,128,128]{2,1,0:T(8,128)(2,1)S(1)}, bf16[8,128,128]{2,1,0:T(8,128)(2,1)S(1)}, u32[]{:S(2)}, u32[]{:S(2)}) collective-permute-start(bf16[8,128,128]{2,1,0:T(8,128)(2,1)S(1)} %get-tuple-element.72), channel_id=1, source_target_pairs={{0,1},{1,0},{2,3},{3,2},{4,5},{5,4},{6,7},{7,6},{8,9},{9,8},{10,11... | collective-permute-start | bytes 786440 | tf_op jit(solution)/shard_map/ppermute | solution.py:462
  53.9 11.3 %collective-permute-start.17 = (bf16[8,128,128]{2,1,0:T(8,128)(2,1)S(1)}, bf16[8,128,128]{2,1,0:T(8,128)(2,1)S(1)}, u32[]{:S(2)}, u32[]{:S(2)}) collective-permute-start(bf16[8,128,128]{2,1,0:T(8,128)(2,1)S(1)} %get-tuple-element.74), channel_id=1, source_target_pairs={{0,2},{1,3},{2,4},{3,5},{4,6},{5,7},{6,8},{7,9},{8,10},{9,11},{10,... | collective-permute-start | bytes 786440 | tf_op jit(solution)/shard_map/ppermute | solution.py:472
  55.6 9.8 %collective-permute-start.21 = (bf16[8,128,128]{2,1,0:T(8,128)(2,1)S(1)}, bf16[8,128,128]{2,1,0:T(8,128)(2,1)S(1)}, u32[]{:S(2)}, u32[]{:S(2)}) collective-permute-start(bf16[8,128,128]{2,1,0:T(8,128)(2,1)S(1)} %get-tuple-element.75), channel_id=1, source_target_pairs={{0,1},{1,0},{2,3},{3,2},{4,5},{5,4},{6,7},{7,6},{8,9},{9,8},{10,11... | collective-permute-start | bytes 786440 | tf_op jit(solution)/shard_map/ppermute | solution.py:462
  57.6 7.9 %collective-permute-start.22 = (bf16[8,128,128]{2,1,0:T(8,128)(2,1)S(1)}, bf16[8,128,128]{2,1,0:T(8,128)(2,1)S(1)}, u32[]{:S(2)}, u32[]{:S(2)}) collective-permute-start(bf16[8,128,128]{2,1,0:T(8,128)(2,1)S(1)} %get-tuple-element.76), channel_id=1, source_target_pairs={{0,14},{1,15},{2,0},{3,1},{4,2},{5,3},{6,4},{7,5},{8,6},{9,7},{10,... | collective-permute-start | bytes 786440 | tf_op jit(solution)/shard_map/ppermute | solution.py:472
  61.6 12.4 %collective-permute-start.14 = (bf16[16,128,128]{2,1,0:T(8,128)(2,1)S(1)}, bf16[16,128,128]{2,1,0:T(8,128)(2,1)S(1)}, u32[]{:S(2)}, u32[]{:S(2)}) collective-permute-start(bf16[16,128,128]{2,1,0:T(8,128)(2,1)S(1)} %get-tuple-element.71), channel_id=1, source_target_pairs={{0,1},{1,0},{2,3},{3,2},{4,5},{5,4},{6,7},{7,6},{8,9},{9,8},{10,11... | collective-permute-start | bytes 1572872 | tf_op jit(solution)/shard_map/ppermute | solution.py:462
  65.3 12.7 %collective-permute-start.18 = (bf16[16,128,128]{2,1,0:T(8,128)(2,1)S(1)}, bf16[16,128,128]{2,1,0:T(8,128)(2,1)S(1)}, u32[]{:S(2)}, u32[]{:S(2)}) collective-permute-start(bf16[16,128,128]{2,1,0:T(8,128)(2,1)S(1)} %hop_3.1), channel_id=1, source_target_pairs={{0,2},{1,3},{2,4},{3,5},{4,6},{5,7},{6,8},{7,9},{8,10},{9,11},{10,... | collective-permute-start | bytes 1572872 | tf_op jit(solution)/shard_map/ppermute | solution.py:472
  65.6 15.4 %collective-permute-start.23 = (bf16[16,128,128]{2,1,0:T(8,128)(2,1)S(1)}, bf16[16,128,128]{2,1,0:T(8,128)(2,1)S(1)}, u32[]{:S(2)}, u32[]{:S(2)}) collective-permute-start(bf16[16,128,128]{2,1,0:T(8,128)(2,1)S(1)} %hop_5.1), channel_id=1, source_target_pairs={{0,14},{1,15},{2,0},{3,1},{4,2},{5,3},{6,4},{7,5},{8,6},{9,7},{10,... | collective-permute-start | bytes 1572872 | tf_op jit(solution)/shard_map/ppermute | solution.py:472
  71.1 15.5 %collective-permute-start.13 = (bf16[16,128,128]{2,1,0:T(8,128)(2,1)S(1)}, bf16[16,128,128]{2,1,0:T(8,128)(2,1)S(1)}, u32[]{:S(2)}, u32[]{:S(2)}) collective-permute-start(bf16[16,128,128]{2,1,0:T(8,128)(2,1)S(1)} %get-tuple-element.70), channel_id=1, source_target_pairs={{0,1},{1,0},{2,3},{3,2},{4,5},{5,4},{6,7},{7,6},{8,9},{9,8},{10,11... | collective-permute-start | bytes 1572872 | tf_op jit(solution)/shard_map/ppermute | solution.py:462
  78.2 14.6 %collective-permute-start.19 = (bf16[16,128,128]{2,1,0:T(8,128)(2,1)S(1)}, bf16[16,128,128]{2,1,0:T(8,128)(2,1)S(1)}, u32[]{:S(2)}, u32[]{:S(2)}) collective-permute-start(bf16[16,128,128]{2,1,0:T(8,128)(2,1)S(1)} %hop_2.1), channel_id=1, source_target_pairs={{0,2},{1,3},{2,4},{3,5},{4,6},{5,7},{6,8},{7,9},{8,10},{9,11},{10,... | collective-permute-start | bytes 1572872 | tf_op jit(solution)/shard_map/ppermute | solution.py:472
  81.2 12.4 %collective-permute-start.24 = (bf16[16,128,128]{2,1,0:T(8,128)(2,1)S(1)}, bf16[16,128,128]{2,1,0:T(8,128)(2,1)S(1)}, u32[]{:S(2)}, u32[]{:S(2)}) collective-permute-start(bf16[16,128,128]{2,1,0:T(8,128)(2,1)S(1)} %hop_6.1), channel_id=1, source_target_pairs={{0,14},{1,15},{2,0},{3,1},{4,2},{5,3},{6,4},{7,5},{8,6},{9,7},{10,... | collective-permute-start | bytes 1572872 | tf_op jit(solution)/shard_map/ppermute | solution.py:472
  93.1 12.3 %copy-start.2 = (bf16[128,256]{1,0:T(8,128)(2,1)S(1)}, bf16[128,256]{1,0:T(8,128)(2,1)}, u32[]{:S(2)}) copy-start(bf16[128,256]{1,0:T(8,128)(2,1)} %weight.1) | copy-start | bytes 196612
  93.1 12.3 %copy-start.3 = (f32[256]{0:T(256)S(1)}, f32[256]{0:T(256)}, u32[]{:S(2)}) copy-start(f32[256]{0:T(256)} %param.13) | copy-start | bytes 3076
  93.1 12.3 %collective-permute-start.20 = (bf16[16,128,128]{2,1,0:T(8,128)(2,1)S(1)}, bf16[16,128,128]{2,1,0:T(8,128)(2,1)S(1)}, u32[]{:S(2)}, u32[]{:S(2)}) collective-permute-start(bf16[16,128,128]{2,1,0:T(8,128)(2,1)S(1)} %hop_1.1), channel_id=1, source_target_pairs={{0,2},{1,3},{2,4},{3,5},{4,6},{5,7},{6,8},{7,9},{8,10},{9,11},{10,... | collective-permute-start | bytes 1572872 | tf_op jit(solution)/shard_map/ppermute | solution.py:485
  93.9 11.5 %collective-permute-start.25 = (bf16[16,128,128]{2,1,0:T(8,128)(2,1)S(1)}, bf16[16,128,128]{2,1,0:T(8,128)(2,1)S(1)}, u32[]{:S(2)}, u32[]{:S(2)}) collective-permute-start(bf16[16,128,128]{2,1,0:T(8,128)(2,1)S(1)} %hop_7.1), channel_id=1, source_target_pairs={{0,14},{1,15},{2,0},{3,1},{4,2},{5,3},{6,4},{7,5},{8,6},{9,7},{10,... | collective-permute-start | bytes 1572872 | tf_op jit(solution)/shard_map/ppermute | solution.py:485
  97.3 6.7 %collective-permute-start.12 = (bf16[8,128,128]{2,1,0:T(8,128)(2,1)S(1)}, bf16[8,128,128]{2,1,0:T(8,128)(2,1)S(1)}, u32[]{:S(2)}, u32[]{:S(2)}) collective-permute-start(bf16[8,128,128]{2,1,0:T(8,128)(2,1)S(1)} %get-tuple-element.69), channel_id=1, source_target_pairs={{0,1},{1,0},{2,3},{3,2},{4,5},{5,4},{6,7},{7,6},{8,9},{9,8},{10,11... | collective-permute-start | bytes 786440 | tf_op jit(solution)/shard_map/ppermute | solution.py:462

commit v3 on v2

--- a/solution.py
+++ b/solution.py
@@ -404,12 +404,22 @@
     )(keep_scalars(slots), keep(own), arrived, *passed)
 
 
-def last_kernel(first, slots, own, arrived, passed_a, passed_b, weight, bias, out):
+def last_kernel(first, slots, own, arrived, passed_a, passed_b, weight, bias, out, held, sems):
+    rows = ROWS // 4
+
+    def copy_out(j):
+        at = pl.ds(j * rows, rows)
+        return pltpu.make_async_copy(held.at[at], out.at[at], sems.at[j])
+
     passed = [(passed_a, 0), (passed_b, 0)]
     for i in range(TPD):
         total = merged(0, first, slots, own, arrived, passed, i).astype(jnp.bfloat16)
         hidden = jnp.dot(total, weight[...], preferred_element_type=jnp.float32) + bias[...]
-        out[pl.ds(i * TILE, TILE), :] = jnp.maximum(hidden, 0.0).astype(out.dtype)
+        held[pl.ds(i * TILE, TILE), :] = jnp.maximum(hidden, 0.0).astype(held.dtype)
+        if (i + 1) * TILE % rows == 0:
+            copy_out(i * TILE // rows).start()
+    for j in range(4):
+        copy_out(j).wait()
 
 
 def last(slots, own, arrived, passed, weight, bias):
@@ -419,7 +429,11 @@
         "last",
         out_shape=jax.ShapeDtypeStruct((ROWS, weight.shape[1]), jnp.bfloat16),
         in_specs=[SMEM_SPEC] + [VMEM_SPEC] * (4 + len(passed)),
-        out_specs=VMEM_SPEC,
+        out_specs=ANY_SPEC,
+        scratch_shapes=[
+            VMEM((ROWS, weight.shape[1]), jnp.bfloat16),
+            pltpu.SemaphoreType.DMA((4,)),
+        ],
     )(keep_scalars(slots), keep(own), part, *passed, weight, bias)
 
 

time: 108 us -> 108 us (level)
  the two profiles are of different devices: /device:TPU:1 before, /device:TPU:24 now
where the time goes in v3:
time: 108 us
  waiting for transfers between devices  47.5 us (44%)
  starting transfers between devices  44 us (41%)
  Pallas kernels  10.3 us (10%)
  local copies, waits for them, and re-layouts  4.62 us (4%)
    ppermute x8, starting transfers between devices, on_device(): chains = [lax.ppermute(c, 'col', p) for c, p in zip(chains, Z_CHAINS)]  19 us
    ppermute x6, waiting for transfers between devices, on_device(): part = lax.ppermute(part, 'col', X_FLIP)  17.3 us
    ppermute x11, waiting for transfers between devices, send(): return lax.ppermute(array, 'row', perm)  14.6 us
    ppermute x8, waiting for transfers between devices, on_device(): chains = [lax.ppermute(c, 'col', p) for c, p in zip(chains, Z_CHAINS)]  13.5 us
    ppermute x6, starting transfers between devices, on_device(): part = lax.ppermute(part, 'col', X_FLIP)  11.9 us
    ppermute x11, starting transfers between devices, send(): return lax.ppermute(array, 'row', perm)  9.6 us
    unnamed x10, local copies, waits for them, and re-layouts  4.54 us
    ppermute x1, starting transfers between devices, on_device(): partner_dest = lax.ppermute(dest, 'col', X_FLIP)  3.56 us
  transfers between devices with their start and end apart: 26, of which 19 were waited for; matrix products, arithmetic and copies ran while one was open for 1% of the time, Pallas kernels for 8%

profile of v3, /device:TPU:24, one launch (start us, length us, event | category | flops | bytes accessed | tf_op | source)
XLA Modules:
  0.0 108.2 jit_solution(17395447823268347734)
XLA Ops:
  0.0 2.0 %collective-permute-start.1 = (bf16[2048,128]{1,0:T(8,128)(2,1)}, bf16[2048,128]{1,0:T(8,128)(2,1)S(1)}, u32[]{:S(2)}, u32[]{:S(2)}) collective-permute-start(bf16[2048,128]{1,0:T(8,128)(2,1)} %refs_0_.1), channel_id=1, source_target_pairs={{0,64},{16,80},{32,96},{48,112},{64,128},{80,144},{96,160},{112,17... | collective-permute-start | bytes 1572872 | tf_op jit(solution)/shard_map/ppermute | solution.py:441
  2.0 1.5 %collective-permute-start.2 = (bf16[2048,128]{1,0:T(8,128)(2,1)}, bf16[2048,128]{1,0:T(8,128)(2,1)S(1)}, u32[]{:S(2)}, u32[]{:S(2)}) collective-permute-start(bf16[2048,128]{1,0:T(8,128)(2,1)} %refs_0_.1), channel_id=1, source_target_pairs={{0,32},{16,48},{32,0},{48,16},{64,96},{80,112},{96,64},{112,80},{1... | collective-permute-start | bytes 1572872 | tf_op jit(solution)/shard_map/ppermute | solution.py:441
  4.2 0.1 stack.23.where
  4.3 0.7 compare_select_fusion.dest
  5.0 0.7 copy-done.4
  5.6 2.4 %plan.1 = (s32[8,512]{1,0:T(8,128)S(4)}, s32[5]{0:T(128)S(1)}) custom-call(s32[5]{0:T(128)S(1)} %stack.23.where, s32[1,256]{1,0:T(1,128)S(1)} %compare_select_fusion.dest, s32[1,256]{1,0:T(1,128)S(1)} %bitcast.14), custom_call_target="tpu_custom_call" | custom-call | tf_op jit(solution)/shard_map/plan/pallas_call | solution.py:162
  8.0 5.9 %collective-permute-done.1.refs_2_ = bf16[2048,128]{1,0:T(8,128)(2,1)S(1)} collective-permute-done((bf16[2048,128]{1,0:T(8,128)(2,1)}, bf16[2048,128]{1,0:T(8,128)(2,1)S(1)}, u32[]{:S(2)}, u32[]{:S(2)}) %collective-permute-start.1) | collective-permute-done | bytes 524320 | tf_op jit(solution)/shard_map/ppermute | solution.py:441
  13.9 1.2 %collective-permute-done.refs_1_ = bf16[2048,128]{1,0:T(8,128)(2,1)S(1)} collective-permute-done((bf16[2048,128]{1,0:T(8,128)(2,1)}, bf16[2048,128]{1,0:T(8,128)(2,1)S(1)}, u32[]{:S(2)}, u32[]{:S(2)}) %collective-permute-start) | collective-permute-done | bytes 524320 | tf_op jit(solution)/shard_map/ppermute | solution.py:441
  15.1 0.3 collective-permute-done.2.refs_3_
  15.3 1.5 %collective-permute-start.4 = (bf16[2048,128]{1,0:T(8,128)(2,1)S(1)}, bf16[2048,128]{1,0:T(8,128)(2,1)S(1)}, u32[]{:S(2)}, u32[]{:S(2)}) collective-permute-start(bf16[2048,128]{1,0:T(8,128)(2,1)S(1)} %collective-permute-done.2.refs_3_), channel_id=1, source_target_pairs={{0,64},{16,80},{32,96},{48,112},{64,128},{80,144},{96,160},{112,17... | collective-permute-start | bytes 1572872 | tf_op jit(solution)/shard_map/ppermute | solution.py:441
  16.8 1.5 %collective-permute-start.5 = (bf16[2048,128]{1,0:T(8,128)(2,1)S(1)}, bf16[2048,128]{1,0:T(8,128)(2,1)S(1)}, u32[]{:S(2)}, u32[]{:S(2)}) collective-permute-start(bf16[2048,128]{1,0:T(8,128)(2,1)S(1)} %collective-permute-done.refs_1_), channel_id=1, source_target_pairs={{0,32},{16,48},{32,0},{48,16},{64,96},{80,112},{96,64},{112,80},{1... | collective-permute-start | bytes 1572872 | tf_op jit(solution)/shard_map/ppermute | solution.py:441
  18.3 0.5 collective-permute-start.3
  18.9 3.4 %copy-done = bf16[1,1,256,128,128]{4,3,2,1,0:T(8,128)(2,1)S(1)} copy-done((bf16[1,1,256,128,128]{4,3,2,1,0:T(8,128)(2,1)S(1)}, bf16[1,1,256,128,128]{4,3,2,1,0:T(8,128)(2,1)}, u32[]{:S(2)}) %copy-start) | copy-done | bytes 8388632
  22.2 0.6 load_tiles.1.tiles
  22.8 0.5 copy-done.1
  23.3 0.1 pack.1.feats
  23.4 1.5 %first_products.1 = (bf16[14336,128]{1,0:T(8,128)(2,1)S(1)}, f32[65,128,128]{2,1,0:T(8,128)S(1)}, f32[129,128,128]{2,1,0:T(8,128)S(1)}) custom-call(s32[8,512]{1,0:T(8,128)S(4)} %get-tuple-element.45.plan, bf16[256,128,128]{2,1,0:T(8,128)(2,1)S(1)} %load_tiles.1.tiles, bf16[14336,128]{1,0:T(8,128)(2,1)S(1)} %pack.1.feats), custom_call_target="tpu_custom_call", output_to_operand_aliasing={{0}: (2, {})} | custom-call | tf_op jit(solution)/shard_map/first_products/pallas_call | solution.py:308
  24.9 2.6 %collective-permute-done.4.down_side = bf16[2048,128]{1,0:T(8,128)(2,1)S(1)} collective-permute-done((bf16[2048,128]{1,0:T(8,128)(2,1)S(1)}, bf16[2048,128]{1,0:T(8,128)(2,1)S(1)}, u32[]{:S(2)}, u32[]{:S(2)}) %collective-permute-start.4) | collective-permute-done | bytes 524320 | tf_op jit(solution)/shard_map/ppermute | solution.py:441
  27.5 0.7 collective-permute-done.5.up_side
  28.3 2.7 %collective-permute-done.3.far = bf16[2048,128]{1,0:T(8,128)(2,1)S(1)} collective-permute-done((bf16[2048,128]{1,0:T(8,128)(2,1)S(1)}, bf16[2048,128]{1,0:T(8,128)(2,1)S(1)}, u32[]{:S(2)}, u32[]{:S(2)}) %collective-permute-start.3) | collective-permute-done | bytes 524320 | tf_op jit(solution)/shard_map/ppermute | solution.py:441
  30.9 0.1 pack_second.1
  31.1 0.1 collective-permute-start.10
  31.3 2.0 %collective-permute-start.6 = (bf16[752,128]{1,0:T(8,128)(2,1)S(1)}, bf16[752,128]{1,0:T(8,128)(2,1)S(1)}, u32[]{:S(2)}, u32[]{:S(2)}) collective-permute-start(bf16[752,128]{1,0:T(8,128)(2,1)S(1)} %get-tuple-element.54), channel_id=1, source_target_pairs={{0,192},{16,208},{32,224},{48,240},{64,0},{80,16},{96,32},{112,48}... | collective-permute-start | bytes 577544 | tf_op jit(solution)/shard_map/ppermute | solution.py:441
  33.3 0.3 collective-permute-start.8
  33.6 3.6 %collective-permute-start.9 = (s32[1,256]{1,0:T(1,128)S(1)}, s32[1,256]{1,0:T(1,128)S(1)}, u32[]{:S(2)}, u32[]{:S(2)}) collective-permute-start(s32[1,256]{1,0:T(1,128)S(1)} %compare_select_fusion.dest), channel_id=1, source_target_pairs={{0,1},{1,0},{2,3},{3,2},{4,5},{5,4},{6,7},{7,6},{8,9},{9,8},{10,11... | collective-permute-start | bytes 3080 | tf_op jit(solution)/shard_map/ppermute | solution.py:461
  37.1 0.6 late_products.1
  37.7 2.1 %collective-permute-done.9.partner_dest = s32[1,256]{1,0:T(1,128)S(1)} collective-permute-done((s32[1,256]{1,0:T(1,128)S(1)}, s32[1,256]{1,0:T(1,128)S(1)}, u32[]{:S(2)}, u32[]{:S(2)}) %collective-permute-start.9) | collective-permute-done | bytes 1056 | tf_op jit(solution)/shard_map/ppermute | solution.py:461
  39.9 0.1 collective-permute-start.11
  40.0 0.6 other_half.1._
  40.7 1.3 %collective-permute-done.11.refs_2_.far_sibling = bf16[2048,128]{1,0:T(8,128)(2,1)S(1)} collective-permute-done((bf16[2048,128]{1,0:T(8,128)(2,1)S(1)}, bf16[2048,128]{1,0:T(8,128)(2,1)S(1)}, u32[]{:S(2)}, u32[]{:S(2)}) %collective-permute-start.11) | collective-permute-done | bytes 524320 | tf_op jit(solution)/shard_map/ppermute | solution.py:441
  42.0 2.8 %collective-permute-start.16 = (bf16[8,128,128]{2,1,0:T(8,128)(2,1)S(1)}, bf16[8,128,128]{2,1,0:T(8,128)(2,1)S(1)}, u32[]{:S(2)}, u32[]{:S(2)}) collective-permute-start(bf16[8,128,128]{2,1,0:T(8,128)(2,1)S(1)} %get-tuple-element.73), channel_id=1, source_target_pairs={{0,1},{1,0},{2,3},{3,2},{4,5},{5,4},{6,7},{7,6},{8,9},{9,8},{10,11... | collective-permute-start | bytes 786440 | tf_op jit(solution)/shard_map/ppermute | solution.py:476
  44.8 1.3 %partner_map.1.slots = s32[1,128]{1,0:T(1,128)S(4)} custom-call(s32[5]{0:T(128)S(1)} %get-tuple-element.42.where, s32[1,256]{1,0:T(1,128)S(1)} %collective-permute-done.9.partner_dest), custom_call_target="tpu_custom_call" | custom-call | tf_op jit(solution)/shard_map/partner_map/pallas_call | solution.py:188
  46.1 0.2 other_sends.1
  46.3 1.1 collective-permute-start.15
  47.3 0.3 own_half.1.own
  47.7 5.0 %collective-permute-done.16.arrived = bf16[8,128,128]{2,1,0:T(8,128)(2,1)S(1)} collective-permute-done((bf16[8,128,128]{2,1,0:T(8,128)(2,1)S(1)}, bf16[8,128,128]{2,1,0:T(8,128)(2,1)S(1)}, u32[]{:S(2)}, u32[]{:S(2)}) %collective-permute-start.16) | collective-permute-done | bytes 262176 | tf_op jit(solution)/shard_map/ppermute | solution.py:476
  52.7 0.1 hop_4.1
  52.8 2.3 %collective-permute-start.17 = (bf16[8,128,128]{2,1,0:T(8,128)(2,1)S(1)}, bf16[8,128,128]{2,1,0:T(8,128)(2,1)S(1)}, u32[]{:S(2)}, u32[]{:S(2)}) collective-permute-start(bf16[8,128,128]{2,1,0:T(8,128)(2,1)S(1)} %get-tuple-element.74), channel_id=1, source_target_pairs={{0,2},{1,3},{2,4},{3,5},{4,6},{5,7},{6,8},{7,9},{8,10},{9,11},{10,... | collective-permute-start | bytes 786440 | tf_op jit(solution)/shard_map/ppermute | solution.py:486
  55.1 2.7 %collective-permute-start.21 = (bf16[8,128,128]{2,1,0:T(8,128)(2,1)S(1)}, bf16[8,128,128]{2,1,0:T(8,128)(2,1)S(1)}, u32[]{:S(2)}, u32[]{:S(2)}) collective-permute-start(bf16[8,128,128]{2,1,0:T(8,128)(2,1)S(1)} %get-tuple-element.75), channel_id=1, source_target_pairs={{0,1},{1,0},{2,3},{3,2},{4,5},{5,4},{6,7},{7,6},{8,9},{9,8},{10,11... | collective-permute-start | bytes 786440 | tf_op jit(solution)/shard_map/ppermute | solution.py:476
  57.9 4.0 %collective-permute-start.22 = (bf16[8,128,128]{2,1,0:T(8,128)(2,1)S(1)}, bf16[8,128,128]{2,1,0:T(8,128)(2,1)S(1)}, u32[]{:S(2)}, u32[]{:S(2)}) collective-permute-start(bf16[8,128,128]{2,1,0:T(8,128)(2,1)S(1)} %get-tuple-element.76), channel_id=1, source_target_pairs={{0,14},{1,15},{2,0},{3,1},{4,2},{5,3},{6,4},{7,5},{8,6},{9,7},{10,... | collective-permute-start | bytes 786440 | tf_op jit(solution)/shard_map/ppermute | solution.py:486
  61.9 0.5 collective-permute-start.14
  62.4 2.0 %collective-permute-done.17.refs_0_ = bf16[8,128,128]{2,1,0:T(8,128)(2,1)S(1)} collective-permute-done((bf16[8,128,128]{2,1,0:T(8,128)(2,1)S(1)}, bf16[8,128,128]{2,1,0:T(8,128)(2,1)S(1)}, u32[]{:S(2)}, u32[]{:S(2)}) %collective-permute-start.17) | collective-permute-done | bytes 262176 | tf_op jit(solution)/shard_map/ppermute | solution.py:486
  64.4 0.2 hop_3.1
  64.6 1.2 %collective-permute-done.22.refs_0_ = bf16[8,128,128]{2,1,0:T(8,128)(2,1)S(1)} collective-permute-done((bf16[8,128,128]{2,1,0:T(8,128)(2,1)S(1)}, bf16[8,128,128]{2,1,0:T(8,128)(2,1)S(1)}, u32[]{:S(2)}, u32[]{:S(2)}) %collective-permute-start.22) | collective-permute-done | bytes 262176 | tf_op jit(solution)/shard_map/ppermute | solution.py:486
  65.9 0.2 hop_5.1
  66.0 4.0 %collective-permute-start.23 = (bf16[16,128,128]{2,1,0:T(8,128)(2,1)S(1)}, bf16[16,128,128]{2,1,0:T(8,128)(2,1)S(1)}, u32[]{:S(2)}, u32[]{:S(2)}) collective-permute-start(bf16[16,128,128]{2,1,0:T(8,128)(2,1)S(1)} %hop_5.1), channel_id=1, source_target_pairs={{0,14},{1,15},{2,0},{3,1},{4,2},{5,3},{6,4},{7,5},{8,6},{9,7},{10,... | collective-permute-start | bytes 1572872 | tf_op jit(solution)/shard_map/ppermute | solution.py:486
  70.0 3.1 %collective-permute-start.13 = (bf16[16,128,128]{2,1,0:T(8,128)(2,1)S(1)}, bf16[16,128,128]{2,1,0:T(8,128)(2,1)S(1)}, u32[]{:S(2)}, u32[]{:S(2)}) collective-permute-start(bf16[16,128,128]{2,1,0:T(8,128)(2,1)S(1)} %get-tuple-element.70), channel_id=1, source_target_pairs={{0,1},{1,0},{2,3},{3,2},{4,5},{5,4},{6,7},{7,6},{8,9},{9,8},{10,11... | collective-permute-start | bytes 1572872 | tf_op jit(solution)/shard_map/ppermute | solution.py:476
  73.1 4.2 %collective-permute-done.14.arrived = bf16[16,128,128]{2,1,0:T(8,128)(2,1)S(1)} collective-permute-done((bf16[16,128,128]{2,1,0:T(8,128)(2,1)S(1)}, bf16[16,128,128]{2,1,0:T(8,128)(2,1)S(1)}, u32[]{:S(2)}, u32[]{:S(2)}) %collective-permute-start.14) | collective-permute-done | bytes 524320 | tf_op jit(solution)/shard_map/ppermute | solution.py:476
  77.3 0.9 collective-permute-done.18.refs_0_
  78.2 0.2 hop_2.1
  78.4 0.9 collective-permute-start.19
  79.3 1.2 %collective-permute-done.23.refs_0_ = bf16[16,128,128]{2,1,0:T(8,128)(2,1)S(1)} collective-permute-done((bf16[16,128,128]{2,1,0:T(8,128)(2,1)S(1)}, bf16[16,128,128]{2,1,0:T(8,128)(2,1)S(1)}, u32[]{:S(2)}, u32[]{:S(2)}) %collective-permute-start.23) | collective-permute-done | bytes 524320 | tf_op jit(solution)/shard_map/ppermute | solution.py:486
  80.5 0.2 hop_6.1
  80.7 3.8 %collective-permute-start.24 = (bf16[16,128,128]{2,1,0:T(8,128)(2,1)S(1)}, bf16[16,128,128]{2,1,0:T(8,128)(2,1)S(1)}, u32[]{:S(2)}, u32[]{:S(2)}) collective-permute-start(bf16[16,128,128]{2,1,0:T(8,128)(2,1)S(1)} %hop_6.1), channel_id=1, source_target_pairs={{0,14},{1,15},{2,0},{3,1},{4,2},{5,3},{6,4},{7,5},{8,6},{9,7},{10,... | collective-permute-start | bytes 1572872 | tf_op jit(solution)/shard_map/ppermute | solution.py:486
  84.5 1.9 %collective-permute-done.13.arrived = bf16[16,128,128]{2,1,0:T(8,128)(2,1)S(1)} collective-permute-done((bf16[16,128,128]{2,1,0:T(8,128)(2,1)S(1)}, bf16[16,128,128]{2,1,0:T(8,128)(2,1)S(1)}, u32[]{:S(2)}, u32[]{:S(2)}) %collective-permute-start.13) | collective-permute-done | bytes 524320 | tf_op jit(solution)/shard_map/ppermute | solution.py:476
  86.4 6.1 %collective-permute-done.19.refs_0_ = bf16[16,128,128]{2,1,0:T(8,128)(2,1)S(1)} collective-permute-done((bf16[16,128,128]{2,1,0:T(8,128)(2,1)S(1)}, bf16[16,128,128]{2,1,0:T(8,128)(2,1)S(1)}, u32[]{:S(2)}, u32[]{:S(2)}) %collective-permute-start.19) | collective-permute-done | bytes 524320 | tf_op jit(solution)/shard_map/ppermute | solution.py:486
  92.5 0.2 hop_1.1
  92.8 1.2 %collective-permute-done.24.refs_0_ = bf16[16,128,128]{2,1,0:T(8,128)(2,1)S(1)} collective-permute-done((bf16[16,128,128]{2,1,0:T(8,128)(2,1)S(1)}, bf16[16,128,128]{2,1,0:T(8,128)(2,1)S(1)}, u32[]{:S(2)}, u32[]{:S(2)}) %collective-permute-start.24) | collective-permute-done | bytes 524320 | tf_op jit(solution)/shard_map/ppermute | solution.py:486
  94.1 0.2 hop_7.1
  94.3 3.8 %collective-permute-start.25 = (bf16[16,128,128]{2,1,0:T(8,128)(2,1)S(1)}, bf16[16,128,128]{2,1,0:T(8,128)(2,1)S(1)}, u32[]{:S(2)}, u32[]{:S(2)}) collective-permute-start(bf16[16,128,128]{2,1,0:T(8,128)(2,1)S(1)} %hop_7.1), channel_id=1, source_target_pairs={{0,14},{1,15},{2,0},{3,1},{4,2},{5,3},{6,4},{7,5},{8,6},{9,7},{10,... | collective-permute-start | bytes 1572872 | tf_op jit(solution)/shard_map/ppermute | solution.py:499
  98.1 1.7 %collective-permute-start.12 = (bf16[8,128,128]{2,1,0:T(8,128)(2,1)S(1)}, bf16[8,128,128]{2,1,0:T(8,128)(2,1)S(1)}, u32[]{:S(2)}, u32[]{:S(2)}) collective-permute-start(bf16[8,128,128]{2,1,0:T(8,128)(2,1)S(1)} %get-tuple-element.69), channel_id=1, source_target_pairs={{0,1},{1,0},{2,3},{3,2},{4,5},{5,4},{6,7},{7,6},{8,9},{9,8},{10,11... | collective-permute-start | bytes 786440 | tf_op jit(solution)/shard_map/ppermute | solution.py:476
  99.8 6.1 %collective-permute-done.12.arrived = bf16[8,128,128]{2,1,0:T(8,128)(2,1)S(1)} collective-permute-done((bf16[8,128,128]{2,1,0:T(8,128)(2,1)S(1)}, bf16[8,128,128]{2,1,0:T(8,128)(2,1)S(1)}, u32[]{:S(2)}, u32[]{:S(2)}) %collective-permute-start.12) | collective-permute-done | bytes 262176 | tf_op jit(solution)/shard_map/ppermute | solution.py:476
  106.0 0.8 collective-permute-done.25.passed_b
  106.7 1.3 %last.1 = bf16[2048,256]{1,0:T(8,128)(2,1)} custom-call(s32[1,128]{1,0:T(1,128)S(4)} %partner_map.1.slots, f32[129,128,128]{2,1,0:T(8,128)S(1)} %own_half.1.own, bf16[8,128,128]{2,1,0:T(8,128)(2,1)S(1)} %collective-permute-done.12.arrived, bf16[16,128,128]{2,1,0:T(8,128)(2,1)S(1)} %collective-permute-done.20.passed_a, ...), custom_call_target="tpu_custom_call" | custom-call | tf_op jit(solution)/shard_map/last/pallas_call | solution.py:427
  (20 shorter events, 0.5 us)
Async XLA Ops:
  0.0 13.9 %collective-permute-start.1 = (bf16[2048,128]{1,0:T(8,128)(2,1)}, bf16[2048,128]{1,0:T(8,128)(2,1)S(1)}, u32[]{:S(2)}, u32[]{:S(2)}) collective-permute-start(bf16[2048,128]{1,0:T(8,128)(2,1)} %refs_0_.1), channel_id=1, source_target_pairs={{0,64},{16,80},{32,96},{48,112},{64,128},{80,144},{96,160},{112,17... | collective-permute-start | bytes 1572872 | tf_op jit(solution)/shard_map/ppermute | solution.py:441
  2.0 13.1 %collective-permute-start = (bf16[2048,128]{1,0:T(8,128)(2,1)}, bf16[2048,128]{1,0:T(8,128)(2,1)S(1)}, u32[]{:S(2)}, u32[]{:S(2)}) collective-permute-start(bf16[2048,128]{1,0:T(8,128)(2,1)} %refs_0_.1), channel_id=1, source_target_pairs={{0,192},{16,208},{32,224},{48,240},{64,0},{80,16},{96,32},{112,48}... | collective-permute-start | bytes 1572872 | tf_op jit(solution)/shard_map/ppermute | solution.py:441
  2.0 13.3 %collective-permute-start.2 = (bf16[2048,128]{1,0:T(8,128)(2,1)}, bf16[2048,128]{1,0:T(8,128)(2,1)S(1)}, u32[]{:S(2)}, u32[]{:S(2)}) collective-permute-start(bf16[2048,128]{1,0:T(8,128)(2,1)} %refs_0_.1), channel_id=1, source_target_pairs={{0,32},{16,48},{32,0},{48,16},{64,96},{80,112},{96,64},{112,80},{1... | collective-permute-start | bytes 1572872 | tf_op jit(solution)/shard_map/ppermute | solution.py:441
  5.0 0.7 copy-start.4
  15.3 12.2 %collective-permute-start.4 = (bf16[2048,128]{1,0:T(8,128)(2,1)S(1)}, bf16[2048,128]{1,0:T(8,128)(2,1)S(1)}, u32[]{:S(2)}, u32[]{:S(2)}) collective-permute-start(bf16[2048,128]{1,0:T(8,128)(2,1)S(1)} %collective-permute-done.2.refs_3_), channel_id=1, source_target_pairs={{0,64},{16,80},{32,96},{48,112},{64,128},{80,144},{96,160},{112,17... | collective-permute-start | bytes 1572872 | tf_op jit(solution)/shard_map/ppermute | solution.py:441
  16.8 11.4 %collective-permute-start.5 = (bf16[2048,128]{1,0:T(8,128)(2,1)S(1)}, bf16[2048,128]{1,0:T(8,128)(2,1)S(1)}, u32[]{:S(2)}, u32[]{:S(2)}) collective-permute-start(bf16[2048,128]{1,0:T(8,128)(2,1)S(1)} %collective-permute-done.refs_1_), channel_id=1, source_target_pairs={{0,32},{16,48},{32,0},{48,16},{64,96},{80,112},{96,64},{112,80},{1... | collective-permute-start | bytes 1572872 | tf_op jit(solution)/shard_map/ppermute | solution.py:441
  18.3 12.6 %collective-permute-start.3 = (bf16[2048,128]{1,0:T(8,128)(2,1)S(1)}, bf16[2048,128]{1,0:T(8,128)(2,1)S(1)}, u32[]{:S(2)}, u32[]{:S(2)}) collective-permute-start(bf16[2048,128]{1,0:T(8,128)(2,1)S(1)} %collective-permute-done.refs_1_), channel_id=1, source_target_pairs={{0,192},{16,208},{32,224},{48,240},{64,0},{80,16},{96,32},{112,48}... | collective-permute-start | bytes 1572872 | tf_op jit(solution)/shard_map/ppermute | solution.py:441
  18.9 3.4 %copy-start = (bf16[1,1,256,128,128]{4,3,2,1,0:T(8,128)(2,1)S(1)}, bf16[1,1,256,128,128]{4,3,2,1,0:T(8,128)(2,1)}, u32[]{:S(2)}) copy-start(bf16[1,1,256,128,128]{4,3,2,1,0:T(8,128)(2,1)} %param.8) | copy-start | bytes 25165828
  22.2 1.0 copy-start.1
  31.1 8.9 %collective-permute-start.10 = (bf16[14336,128]{1,0:T(8,128)(2,1)S(1)}, bf16[14336,128]{1,0:T(8,128)(2,1)S(1)}, u32[]{:S(2)}, u32[]{:S(2)}) collective-permute-start(bf16[14336,128]{1,0:T(8,128)(2,1)S(1)} %get-tuple-element.57.refs_0_), channel_id=1, source_target_pairs={{0,16},{16,0},{32,48},{48,32},{64,80},{80,64},{96,112},{112,96},{1... | collective-permute-start | bytes 11010056 | tf_op jit(solution)/shard_map/ppermute | solution.py:441
  31.2 8.7 %collective-permute-start.7 = (bf16[880,128]{1,0:T(8,128)(2,1)S(1)}, bf16[880,128]{1,0:T(8,128)(2,1)S(1)}, u32[]{:S(2)}, u32[]{:S(2)}) collective-permute-start(bf16[880,128]{1,0:T(8,128)(2,1)S(1)} %get-tuple-element.55), channel_id=1, source_target_pairs={{0,64},{16,80},{32,96},{48,112},{64,128},{80,144},{96,160},{112,17... | collective-permute-start | bytes 675848 | tf_op jit(solution)/shard_map/ppermute | solution.py:441
  31.3 8.6 %collective-permute-start.6 = (bf16[752,128]{1,0:T(8,128)(2,1)S(1)}, bf16[752,128]{1,0:T(8,128)(2,1)S(1)}, u32[]{:S(2)}, u32[]{:S(2)}) collective-permute-start(bf16[752,128]{1,0:T(8,128)(2,1)S(1)} %get-tuple-element.54), channel_id=1, source_target_pairs={{0,192},{16,208},{32,224},{48,240},{64,0},{80,16},{96,32},{112,48}... | collective-permute-start | bytes 577544 | tf_op jit(solution)/shard_map/ppermute | solution.py:441
  33.3 6.6 %collective-permute-start.8 = (bf16[416,128]{1,0:T(8,128)(2,1)S(1)}, bf16[416,128]{1,0:T(8,128)(2,1)S(1)}, u32[]{:S(2)}, u32[]{:S(2)}) collective-permute-start(bf16[416,128]{1,0:T(8,128)(2,1)S(1)} %get-tuple-element.56), channel_id=1, source_target_pairs={{0,32},{16,48},{32,0},{48,16},{64,96},{80,112},{96,64},{112,80},{1... | collective-permute-start | bytes 319496 | tf_op jit(solution)/shard_map/ppermute | solution.py:441
  33.6 6.3 %collective-permute-start.9 = (s32[1,256]{1,0:T(1,128)S(1)}, s32[1,256]{1,0:T(1,128)S(1)}, u32[]{:S(2)}, u32[]{:S(2)}) collective-permute-start(s32[1,256]{1,0:T(1,128)S(1)} %compare_select_fusion.dest), channel_id=1, source_target_pairs={{0,1},{1,0},{2,3},{3,2},{4,5},{5,4},{6,7},{7,6},{8,9},{9,8},{10,11... | collective-permute-start | bytes 3080 | tf_op jit(solution)/shard_map/ppermute | solution.py:461
  39.9 2.0 %collective-permute-start.11 = (bf16[2048,128]{1,0:T(8,128)(2,1)S(1)}, bf16[2048,128]{1,0:T(8,128)(2,1)S(1)}, u32[]{:S(2)}, u32[]{:S(2)}) collective-permute-start(bf16[2048,128]{1,0:T(8,128)(2,1)S(1)} %join.1.refs_1_), channel_id=1, source_target_pairs={{0,16},{16,0},{32,48},{48,32},{64,80},{80,64},{96,112},{112,96},{1... | collective-permute-start | bytes 1572872 | tf_op jit(solution)/shard_map/ppermute | solution.py:441
  42.0 10.7 %collective-permute-start.16 = (bf16[8,128,128]{2,1,0:T(8,128)(2,1)S(1)}, bf16[8,128,128]{2,1,0:T(8,128)(2,1)S(1)}, u32[]{:S(2)}, u32[]{:S(2)}) collective-permute-start(bf16[8,128,128]{2,1,0:T(8,128)(2,1)S(1)} %get-tuple-element.73), channel_id=1, source_target_pairs={{0,1},{1,0},{2,3},{3,2},{4,5},{5,4},{6,7},{7,6},{8,9},{9,8},{10,11... | collective-permute-start | bytes 786440 | tf_op jit(solution)/shard_map/ppermute | solution.py:476
  46.3 16.1 %collective-permute-start.15 = (bf16[8,128,128]{2,1,0:T(8,128)(2,1)S(1)}, bf16[8,128,128]{2,1,0:T(8,128)(2,1)S(1)}, u32[]{:S(2)}, u32[]{:S(2)}) collective-permute-start(bf16[8,128,128]{2,1,0:T(8,128)(2,1)S(1)} %get-tuple-element.72), channel_id=1, source_target_pairs={{0,1},{1,0},{2,3},{3,2},{4,5},{5,4},{6,7},{7,6},{8,9},{9,8},{10,11... | collective-permute-start | bytes 786440 | tf_op jit(solution)/shard_map/ppermute | solution.py:476
  52.8 11.6 %collective-permute-start.17 = (bf16[8,128,128]{2,1,0:T(8,128)(2,1)S(1)}, bf16[8,128,128]{2,1,0:T(8,128)(2,1)S(1)}, u32[]{:S(2)}, u32[]{:S(2)}) collective-permute-start(bf16[8,128,128]{2,1,0:T(8,128)(2,1)S(1)} %get-tuple-element.74), channel_id=1, source_target_pairs={{0,2},{1,3},{2,4},{3,5},{4,6},{5,7},{6,8},{7,9},{8,10},{9,11},{10,... | collective-permute-start | bytes 786440 | tf_op jit(solution)/shard_map/ppermute | solution.py:486
  55.1 9.5 %collective-permute-start.21 = (bf16[8,128,128]{2,1,0:T(8,128)(2,1)S(1)}, bf16[8,128,128]{2,1,0:T(8,128)(2,1)S(1)}, u32[]{:S(2)}, u32[]{:S(2)}) collective-permute-start(bf16[8,128,128]{2,1,0:T(8,128)(2,1)S(1)} %get-tuple-element.75), channel_id=1, source_target_pairs={{0,1},{1,0},{2,3},{3,2},{4,5},{5,4},{6,7},{7,6},{8,9},{9,8},{10,11... | collective-permute-start | bytes 786440 | tf_op jit(solution)/shard_map/ppermute | solution.py:476
  57.9 8.0 %collective-permute-start.22 = (bf16[8,128,128]{2,1,0:T(8,128)(2,1)S(1)}, bf16[8,128,128]{2,1,0:T(8,128)(2,1)S(1)}, u32[]{:S(2)}, u32[]{:S(2)}) collective-permute-start(bf16[8,128,128]{2,1,0:T(8,128)(2,1)S(1)} %get-tuple-element.76), channel_id=1, source_target_pairs={{0,14},{1,15},{2,0},{3,1},{4,2},{5,3},{6,4},{7,5},{8,6},{9,7},{10,... | collective-permute-start | bytes 786440 | tf_op jit(solution)/shard_map/ppermute | solution.py:486
  61.9 15.4 %collective-permute-start.14 = (bf16[16,128,128]{2,1,0:T(8,128)(2,1)S(1)}, bf16[16,128,128]{2,1,0:T(8,128)(2,1)S(1)}, u32[]{:S(2)}, u32[]{:S(2)}) collective-permute-start(bf16[16,128,128]{2,1,0:T(8,128)(2,1)S(1)} %get-tuple-element.71), channel_id=1, source_target_pairs={{0,1},{1,0},{2,3},{3,2},{4,5},{5,4},{6,7},{7,6},{8,9},{9,8},{10,11... | collective-permute-start | bytes 1572872 | tf_op jit(solution)/shard_map/ppermute | solution.py:476
  64.5 13.7 %collective-permute-start.18 = (bf16[16,128,128]{2,1,0:T(8,128)(2,1)S(1)}, bf16[16,128,128]{2,1,0:T(8,128)(2,1)S(1)}, u32[]{:S(2)}, u32[]{:S(2)}) collective-permute-start(bf16[16,128,128]{2,1,0:T(8,128)(2,1)S(1)} %hop_3.1), channel_id=1, source_target_pairs={{0,2},{1,3},{2,4},{3,5},{4,6},{5,7},{6,8},{7,9},{8,10},{9,11},{10,... | collective-permute-start | bytes 1572872 | tf_op jit(solution)/shard_map/ppermute | solution.py:486
  66.0 14.5 %collective-permute-start.23 = (bf16[16,128,128]{2,1,0:T(8,128)(2,1)S(1)}, bf16[16,128,128]{2,1,0:T(8,128)(2,1)S(1)}, u32[]{:S(2)}, u32[]{:S(2)}) collective-permute-start(bf16[16,128,128]{2,1,0:T(8,128)(2,1)S(1)} %hop_5.1), channel_id=1, source_target_pairs={{0,14},{1,15},{2,0},{3,1},{4,2},{5,3},{6,4},{7,5},{8,6},{9,7},{10,... | collective-permute-start | bytes 1572872 | tf_op jit(solution)/shard_map/ppermute | solution.py:486
  70.0 16.4 %collective-permute-start.13 = (bf16[16,128,128]{2,1,0:T(8,128)(2,1)S(1)}, bf16[16,128,128]{2,1,0:T(8,128)(2,1)S(1)}, u32[]{:S(2)}, u32[]{:S(2)}) collective-permute-start(bf16[16,128,128]{2,1,0:T(8,128)(2,1)S(1)} %get-tuple-element.70), channel_id=1, source_target_pairs={{0,1},{1,0},{2,3},{3,2},{4,5},{5,4},{6,7},{7,6},{8,9},{9,8},{10,11... | collective-permute-start | bytes 1572872 | tf_op jit(solution)/shard_map/ppermute | solution.py:476
  78.4 14.1 %collective-permute-start.19 = (bf16[16,128,128]{2,1,0:T(8,128)(2,1)S(1)}, bf16[16,128,128]{2,1,0:T(8,128)(2,1)S(1)}, u32[]{:S(2)}, u32[]{:S(2)}) collective-permute-start(bf16[16,128,128]{2,1,0:T(8,128)(2,1)S(1)} %hop_2.1), channel_id=1, source_target_pairs={{0,2},{1,3},{2,4},{3,5},{4,6},{5,7},{6,8},{7,9},{8,10},{9,11},{10,... | collective-permute-start | bytes 1572872 | tf_op jit(solution)/shard_map/ppermute | solution.py:486
  80.7 13.4 %collective-permute-start.24 = (bf16[16,128,128]{2,1,0:T(8,128)(2,1)S(1)}, bf16[16,128,128]{2,1,0:T(8,128)(2,1)S(1)}, u32[]{:S(2)}, u32[]{:S(2)}) collective-permute-start(bf16[16,128,128]{2,1,0:T(8,128)(2,1)S(1)} %hop_6.1), channel_id=1, source_target_pairs={{0,14},{1,15},{2,0},{3,1},{4,2},{5,3},{6,4},{7,5},{8,6},{9,7},{10,... | collective-permute-start | bytes 1572872 | tf_op jit(solution)/shard_map/ppermute | solution.py:486
  92.7 14.0 %copy-start.2 = (bf16[128,256]{1,0:T(8,128)(2,1)S(1)}, bf16[128,256]{1,0:T(8,128)(2,1)}, u32[]{:S(2)}) copy-start(bf16[128,256]{1,0:T(8,128)(2,1)} %weight.1) | copy-start | bytes 196612
  92.7 14.0 %copy-start.3 = (f32[256]{0:T(256)S(1)}, f32[256]{0:T(256)}, u32[]{:S(2)}) copy-start(f32[256]{0:T(256)} %param.13) | copy-start | bytes 3076
  92.8 13.2 %collective-permute-start.20 = (bf16[16,128,128]{2,1,0:T(8,128)(2,1)S(1)}, bf16[16,128,128]{2,1,0:T(8,128)(2,1)S(1)}, u32[]{:S(2)}, u32[]{:S(2)}) collective-permute-start(bf16[16,128,128]{2,1,0:T(8,128)(2,1)S(1)} %hop_1.1), channel_id=1, source_target_pairs={{0,2},{1,3},{2,4},{3,5},{4,6},{5,7},{6,8},{7,9},{8,10},{9,11},{10,... | collective-permute-start | bytes 1572872 | tf_op jit(solution)/shard_map/ppermute | solution.py:499
  94.3 12.4 %collective-permute-start.25 = (bf16[16,128,128]{2,1,0:T(8,128)(2,1)S(1)}, bf16[16,128,128]{2,1,0:T(8,128)(2,1)S(1)}, u32[]{:S(2)}, u32[]{:S(2)}) collective-permute-start(bf16[16,128,128]{2,1,0:T(8,128)(2,1)S(1)} %hop_7.1), channel_id=1, source_target_pairs={{0,14},{1,15},{2,0},{3,1},{4,2},{5,3},{6,4},{7,5},{8,6},{9,7},{10,... | collective-permute-start | bytes 1572872 | tf_op jit(solution)/shard_map/ppermute | solution.py:499
  98.1 7.9 %collective-permute-start.12 = (bf16[8,128,128]{2,1,0:T(8,128)(2,1)S(1)}, bf16[8,128,128]{2,1,0:T(8,128)(2,1)S(1)}, u32[]{:S(2)}, u32[]{:S(2)}) collective-permute-start(bf16[8,128,128]{2,1,0:T(8,128)(2,1)S(1)} %get-tuple-element.69), channel_id=1, source_target_pairs={{0,1},{1,0},{2,3},{3,2},{4,5},{5,4},{6,7},{7,6},{8,9},{9,8},{10,11... | collective-permute-start | bytes 786440 | tf_op jit(solution)/shard_map/ppermute | solution.py:476
